TPU v7x, 256 devices: a whole 4x4x8 slice. The times are simulated.
256 devices in a mesh: ctx: 16 (over x, y), head: 8 (over z), fsdp: 2 (over core).
Axes of the slice: x: 4, y: 4, z: 8, core: 2. Of those that a mesh axis runs over, the one named last changes fastest.
Arguments:
- layer_input: bfloat16 [16384, 4096], P(('ctx', 'fsdp')), may hold values from -6 to 6
- query_act: bfloat16 [16384, 4096], P(('ctx', 'fsdp'), 'head'), may hold values from -6 to 6
- key_act: bfloat16 [16384, 4096], P(('ctx', 'fsdp'), 'head'), may hold values from -6 to 6
- out_grad: bfloat16 [16384, 4096], P(('ctx', 'fsdp'), 'head'), may hold values from -6 to 6
- value_weight: bfloat16 [4096, 4096], P('fsdp', 'head'), may hold values from -0.09375 to 0.09375
Outputs:
- query_grad: bfloat16 [16384, 4096], P(('ctx', 'fsdp'), 'head')
- key_grad: bfloat16 [16384, 4096], P(('ctx', 'fsdp'), 'head')
- input_grad: bfloat16 [16384, 4096], P(('ctx', 'fsdp'), 'head')
- weight_grad: float32 [4096, 4096], P(('ctx', 'fsdp'), 'head')
All inputs are finite; a program needn't handle non-finite values.
Results may differ from a plain program's by a relative error of at most 0.018.
Values may be sent and summed in bfloat16 or wider, within the bound.
No kernel may reach another device: no remote copies, remote signals or barrier semaphores. Data moves between devices by JAX's collectives and lax.ppermute only.
A program may use at most 64 MiB of HBM per device.

v0:
```python
import math

import jax
import jax.numpy as jnp
from jax import lax
from jax.sharding import PartitionSpec as P

HDIM = 128


def entering(array, axis, join, neutral):
    place = lax.axis_index(axis)
    gathered = lax.all_gather(array.astype(jnp.bfloat16), axis)
    state = jnp.zeros_like(array) + jnp.asarray(neutral, array.dtype)

    def one(step, state):
        return join(state, lax.dynamic_index_in_dim(gathered, step, 0, False).astype(array.dtype))

    return lax.fori_loop(0, place, one, state)


def entering_2(array, axis, join, neutral):
    count = lax.axis_size(axis)
    place = lax.axis_index(axis)
    ahead = count - 1 - place
    gathered = lax.all_gather(
        array.astype(jnp.bfloat16 if array.dtype == jnp.float32 else array.dtype), axis
    )
    state = jnp.zeros_like(array) + jnp.asarray(neutral, array.dtype)

    def one(step, state):
        source = count - 1 - step
        return join(state, lax.dynamic_index_in_dim(gathered, source, 0, False).astype(array.dtype))

    return lax.fori_loop(0, ahead, one, state)


def product(pattern, former, latter):
    return jnp.einsum(pattern, former, latter, precision=lax.Precision.HIGHEST)


def lowdot(pattern, former, latter):
    return jnp.einsum(pattern, former, latter, preferred_element_type=jnp.float32)


def add_states(earlier, following):
    return earlier + following


def norm_grad(attended, grad_heads):
    inverse_rms = lax.rsqrt(jnp.mean(attended * attended, axis=-1, keepdims=True) + 1e-05)
    normed = attended * inverse_rms
    return inverse_rms * (
        grad_heads - normed * jnp.mean(grad_heads * normed, axis=-1, keepdims=True)
    )


def local(layer_input, query_act, key_act, out_grad, value_weight):
    tok_rows = layer_input.shape[0]
    weight_full = lax.all_gather(value_weight, "fsdp", axis=0, tiled=True)
    value_act = jnp.dot(layer_input, weight_full, preferred_element_type=jnp.float32).astype(
        jnp.bfloat16
    )
    heads_dev = query_act.shape[1] // HDIM
    head_shape = (tok_rows, heads_dev, HDIM)
    query_heads = query_act.reshape(head_shape)
    key_heads = key_act.reshape(head_shape)
    value_heads = value_act.reshape(head_shape)
    query_wide = query_heads.astype(jnp.float32)
    key_wide = key_heads.astype(jnp.float32)
    value_wide = value_heads.astype(jnp.float32)
    grad_wide = out_grad.reshape(head_shape).astype(jnp.float32)
    pair_sum = lowdot("shi,shj->hij", key_heads, value_heads)
    state_prev = entering(pair_sum, ("ctx", "fsdp"), add_states, jnp.zeros_like(pair_sum))
    causal = jnp.tril(jnp.ones((tok_rows, tok_rows), dtype=bool))
    scores = lowdot("thi,shi->hts", query_heads, key_heads)
    masked = jnp.where(causal[None], scores, 0.0).astype(jnp.bfloat16)
    attended = lowdot("hts,shj->thj", masked, value_heads) + product(
        "thi,hij->thj", query_wide, state_prev
    )
    attn_grad = norm_grad(attended, grad_wide)
    attn_low = attn_grad.astype(jnp.bfloat16)
    local_grad = product("thi,thj->hij", query_wide, attn_grad)
    state_grad = entering_2(local_grad, ("ctx", "fsdp"), add_states, jnp.zeros_like(local_grad))
    cross_terms = jnp.where(
        causal[None], lowdot("thj,shj->hts", attn_low, value_heads), 0.0
    ).astype(jnp.bfloat16)
    query_part = lowdot("hts,shi->thi", cross_terms, key_heads) + product(
        "hij,thj->thi", state_prev, attn_grad
    )
    key_part = lowdot("hts,thi->shi", cross_terms, query_heads) + product(
        "hij,shj->shi", state_grad, value_wide
    )
    value_part = lowdot("hts,thj->shj", masked, attn_low) + product(
        "shi,hij->shj", key_wide, state_grad
    )
    query_grad = query_part.reshape(tok_rows, -1).astype(jnp.bfloat16)
    key_grad = key_part.reshape(tok_rows, -1).astype(jnp.bfloat16)
    value_grad = value_part.reshape(tok_rows, -1).astype(jnp.bfloat16)
    seq_devices = lax.axis_size(("ctx", "fsdp"))
    grad_scale = 1.0 / math.sqrt(tok_rows * seq_devices)
    weight_grad = lax.psum_scatter(
        (
            lax.dot_general(
                layer_input,
                value_grad,
                (((0,), (0,)), ((), ())),
                preferred_element_type=jnp.float32,
            )
            * grad_scale
        ).astype(jnp.bfloat16),
        ("ctx", "fsdp"),
        scatter_dimension=0,
        tiled=True,
    ).astype(jnp.float32)
    partial_input = lax.dot_general(
        value_grad, weight_full, (((1,), (1,)), ((), ())), preferred_element_type=jnp.float32
    )
    input_grad = lax.psum_scatter(
        partial_input.astype(jnp.bfloat16), "head", scatter_dimension=1, tiled=True
    )
    return (query_grad, key_grad, input_grad, weight_grad)


def solution(mesh):
    in_specs = (
        P(("ctx", "fsdp"), None),
        P(("ctx", "fsdp"), "head"),
        P(("ctx", "fsdp"), "head"),
        P(("ctx", "fsdp"), "head"),
        P("fsdp", "head"),
    )
    out_specs = (
        P(("ctx", "fsdp"), "head"),
        P(("ctx", "fsdp"), "head"),
        P(("ctx", "fsdp"), "head"),
        P(("ctx", "fsdp"), "head"),
    )
    return jax.shard_map(local, mesh=mesh, in_specs=in_specs, out_specs=out_specs, check_vma=False)
```

profile of v0, /device:TPU:24, one launch (start us, length us, event | category | flops | bytes accessed | tf_op | source)
XLA Modules:
  0.0 370.8 jit_solution(7606980007182859887)
XLA Ops:
  8.0 23.6 %all-gather.6.cloned.1.call-done = bf16[4096,512]{1,0:T(8,128)(2,1)} async-done(((bf16[2048,512]{1,0:T(8,128)(2,1)}), bf16[4096,512]{1,0:T(8,128)(2,1)}) %all-gather.6.cloned.1.call-update) | async-done | bytes 4194320 | tf_op jit(solution)/shard_map/all_gather | solution.py:60
  31.6 5.8 %convolution_convert_fusion.1 = bf16[512,512]{0,1:T(8,128)(2,1)S(1)} fusion(bf16[512,4096]{1,0:T(8,128)(2,1)} %param.9, bf16[4096,512]{1,0:T(8,128)(2,1)} %all-gather.6.cloned.1.call-done), kind=kOutput, calls=%fused_computation.12 | convolution fusion | flops 2147745792 | bytes 8912896 | tf_op jit(solution)/shard_map/dot_general | solution.py:61
  39.6 1.4 copy-done.2
  41.8 48.8 %all-gather.8.cloned.1.call-done = bf16[128,128,128]{2,1,0:T(8,128)(2,1)} async-done(((bf16[4,128,128]{2,1,0:T(8,128)(2,1)}), bf16[128,128,128]{2,1,0:T(8,128)(2,1)}) %all-gather.8.cloned.1.call-update) | async-done | bytes 4194320 | tf_op jit(solution)/shard_map/all_gather | solution.py:13
  90.7 5.9 %while.22 = (s32[]{:T(128)}, f32[4,128,128]{2,1,0:T(8,128)S(1)}, s32[]{:T(128)}, bf16[32,4,128,128]{3,2,1,0:T(8,128)(2,1)}, s32[]{:T(128)}, /*index=5*/s32[]{:T(128)}, s32[]{:T(128)}) while((s32[]{:T(128)}, f32[4,128,128]{2,1,0:T(8,128)S(1)}, s32[]{:T(128)}, bf16[32,4,128,128]{3,2,1,0:T(8,128)(2,1)}, s32[]{:T(128)}, /*index=5*/s32[]{:T(128)}, ...), condition=%wide.region_1.2_spmd, body=%wide.region_0.1_spmd.sunk | while | flops 131077 | bytes 655483 | solution.py:19
  99.4 3.0 fusion.25
  102.4 71.2 %all-gather.10.cloned.1.call-done = bf16[128,128,128]{2,1,0:T(8,128)(2,1)} async-done(((bf16[4,128,128]{2,1,0:T(8,128)(2,1)}), bf16[128,128,128]{2,1,0:T(8,128)(2,1)}) %all-gather.10.cloned.1.call-update) | async-done | bytes 4194320 | tf_op jit(solution)/shard_map/all_gather | solution.py:26
  173.7 24.7 %while.23 = (s32[]{:T(128)}, f32[4,128,128]{2,1,0:T(8,128)S(1)}, s32[]{:T(128)}, bf16[32,4,128,128]{3,2,1,0:T(8,128)(2,1)}, s32[]{:T(128)}, /*index=5*/s32[]{:T(128)}, s32[]{:T(128)}, s32[]{:T(128)}) while((s32[]{:T(128)}, f32[4,128,128]{2,1,0:T(8,128)S(1)}, s32[]{:T(128)}, bf16[32,4,128,128]{3,2,1,0:T(8,128)(2,1)}, s32[]{:T(128)}, ...), condition=%wide.region_5.6_spmd, body=%wide.region_4.5_spmd.sunk | while | flops 131078 | bytes 655503 | solution.py:35
  173.7 1.0 convert_add_fusion.5
  174.7 1.0 convert_add_fusion.5
  175.7 1.0 convert_add_fusion.5
  176.7 1.0 convert_add_fusion.5
  177.6 1.0 convert_add_fusion.5
  198.4 1.8 fusion.4
  201.0 6.5 %fusion = bf16[4096,512]{0,1:T(8,128)(2,1)} fusion(bf16[512,512]{0,1:T(8,128)(2,1)S(1)} %bitcast.106, bf16[512,4096]{1,0:T(8,128)(2,1)} %param.9), kind=kOutput, calls=%fused_computation.4 | convolution fusion | flops 2151677952 | bytes 8912896 | tf_op jit(solution)/shard_map/dot_general | solution.py:104
  207.5 6.5 %copy.55 = bf16[4096,512]{1,0:T(8,128)(2,1)} copy(bf16[4096,512]{0,1:T(8,128)(2,1)} %fusion) | data formatting | bytes 8388608
  214.2 6.7 %convolution_convert_fusion = bf16[512,4096]{1,0:T(8,128)(2,1)} fusion(bf16[512,512]{0,1:T(8,128)(2,1)} %bitcast.107, bf16[4096,512]{1,0:T(8,128)(2,1)} %all-gather.6.cloned.1.call-done), kind=kOutput, calls=%fused_computation.3 | convolution fusion | flops 2149580800 | bytes 8912896 | tf_op jit(solution)/shard_map/dot_general | solution.py:116
  223.6 1.1 fusion.2
  224.7 1.0 copy.46
  225.7 2.1 fusion.12
  228.3 1.0 copy.47
  229.3 76.7 %reduce-scatter.7.cloned.1.call-done = bf16[128,512]{1,0:T(8,128)(2,1)} async-done(((bf16[4096,512]{1,0:T(8,128)(2,1)}), bf16[128,512]{1,0:T(8,128)(2,1)}) %reduce-scatter.7.cloned.1.call-update) | async-done | bytes 131088
  306.1 1.0 copy.56
  307.9 56.4 %reduce-scatter.5.cloned.1.call-done = bf16[512,512]{1,0:T(8,128)(2,1)} async-done(((bf16[512,4096]{1,0:T(8,128)(2,1)}), bf16[512,512]{1,0:T(8,128)(2,1)}) %reduce-scatter.5.cloned.1.call-update) | async-done | bytes 524304 | tf_op jit(solution)/shard_map/reduce_scatter | solution.py:119
  (72 shorter events, 36.5 us)
Async XLA Ops:
  7.2 31.7 %copy-start = (bf16[512,512]{1,0:T(8,128)(2,1)S(1)}, bf16[512,512]{1,0:T(8,128)(2,1)}, u32[]{:S(2)}) copy-start(bf16[512,512]{1,0:T(8,128)(2,1)} %param.10) | copy-start | bytes 1572868
  7.2 24.4 %all-gather.6.cloned.1.call-start = ((), (), s32[]{:S(2)}) async-start(), calls=%async_computation.2 | async-start | bytes 6291456 | tf_op jit(solution)/shard_map/all_gather | solution.py:60
  7.9 29.5 %copy-start.3 = (bf16[512,512]{1,0:T(8,128)(2,1)S(1)}, bf16[512,512]{1,0:T(8,128)(2,1)}, u32[]{:S(2)}) copy-start(bf16[512,512]{1,0:T(8,128)(2,1)} %param.11) | copy-start | bytes 1572868
  7.9 30.6 %copy-start.7 = (bf16[512,512]{1,0:T(8,128)(2,1)S(1)}, bf16[512,512]{1,0:T(8,128)(2,1)}, u32[]{:S(2)}) copy-start(bf16[512,512]{1,0:T(8,128)(2,1)} %param.12) | copy-start | bytes 1572868
  7.9 82.7 %all-gather.8.cloned.1.call-start = ((), (), s32[]{:S(2)}) async-start(), calls=%async_computation.4 | async-start | bytes 4325376 | tf_op jit(solution)/shard_map/all_gather | solution.py:13
  38.5 135.2 %all-gather.10.cloned.1.call-start = ((), (), s32[]{:S(2)}) async-start(), calls=%async_computation.5 | async-start | bytes 4325376 | tf_op jit(solution)/shard_map/all_gather | solution.py:26
  38.9 51.8 %copy-start.5 = (pred[512,512]{1,0:T(8,128)(4,1)}, pred[512,512]{1,0:T(8,128)(4,1)S(1)}, u32[]{:S(2)}) copy-start(pred[512,512]{1,0:T(8,128)(4,1)S(1)} %iota_compare_fusion) | copy-start | bytes 786436
  39.6 1.4 copy-start.2
  98.5 99.8 %copy-start.4 = (bf16[512,512]{1,0:T(8,128)(2,1)S(1)}, bf16[512,512]{1,0:T(8,128)(2,1)}, u32[]{:S(2)}) copy-start(bf16[512,512]{1,0:T(8,128)(2,1)} %param.11) | copy-start | bytes 1572868
  99.3 206.7 %reduce-scatter.7.cloned.1.call-start = ((), (), s32[]{:S(2)}) async-start(), calls=%async_computation.6 | async-start | bytes 4325376
  200.2 0.8 copy-start.8
  214.0 150.3 %reduce-scatter.5.cloned.1.call-start = ((), (), s32[]{:S(2)}) async-start(), calls=%async_computation.3 | async-start | bytes 4718592 | tf_op jit(solution)/shard_map/reduce_scatter | solution.py:119
  221.0 0.9 copy-start.6
  222.7 1.9 copy-start.1
Sparse Core Ops, SparseCore 0:
  9.8 21.6 all-gather.5
  38.6 51.9 all-gather.7
  99.4 74.1 all-gather.9
  214.1 91.8 reduce-scatter.6
  309.2 55.0 reduce-scatter.4
where the time goes:
time: 373 us; the launch traced here: 371 us
  waiting for transfers between devices  277 us (74%)
  matrix products  32.4 us (9%)
  other arithmetic  30.5 us (8%)
  local copies, waits for them, and re-layouts  15.2 us (4%)
  between operations  14 us (4%)
    unnamed x6, waiting for transfers between devices  77.5 us
    all_gather x1, waiting for transfers between devices, entering_2(): lax.all_gather(array.astype(jnp.bfloat16 if array.dtype == jnp.float32 el...  71.2 us
    reduce_scatter x1, waiting for transfers between devices, local(): lax.psum_scatter(partial_input.astype(jnp.bfloat16), 'head', scatter_dime...  56.4 us
    all_gather x1, waiting for transfers between devices, entering(): gathered = lax.all_gather(array.astype(jnp.bfloat16), axis)  48.8 us
    add x31, other arithmetic, add_states(): return earlier + following  29.9 us
    all_gather x1, waiting for transfers between devices, local(): weight_full = lax.all_gather(value_weight, 'fsdp', axis=0, tiled=True)  23.6 us
    unnamed x23, local copies, waits for them, and re-layouts  13.4 us
    dot_general x7, matrix products, lowdot(): jnp.einsum(pattern, former, latter, preferred_element_type=jnp.float32)  8.56 us
  transfers between devices with their start and end apart: 5, of which 5 were waited for; matrix products, arithmetic and copies ran while one was open for 6% of the time, Pallas kernels for 0%

commit v1 on v0

v1 whole, which is shorter than its diff:
```python
import math

import jax
import jax.numpy as jnp
from jax import lax
from jax.experimental import pallas as pl
from jax.experimental.pallas import tpu as pltpu
from jax.sharding import PartitionSpec as P

HDIM = 128
F32 = jnp.float32
BF16 = jnp.bfloat16
NT = (((1,), (1,)), ((), ()))
TN = (((0,), (0,)), ((), ()))
NN = (((1,), (0,)), ((), ()))


def dot(a, b, dims=NN):
    return lax.dot_general(a, b, dims, preferred_element_type=F32)


def params(**more):
    return pltpu.CompilerParams(vmem_limit_bytes=40 * 2**20, **more)


def cost(flops, nbytes):
    return pl.CostEstimate(flops=int(flops), bytes_accessed=int(nbytes), transcendentals=0)


def sds(shape, dtype):
    return jax.ShapeDtypeStruct(shape, dtype)


def value_own_kernel(core, x_ref, w_ref, o_ref):
    prod = dot(x_ref[...], w_ref[...])

    @pl.when(pl.program_id(0) == 0)
    def _():
        o_ref[...] = prod

    @pl.when(pl.program_id(0) > 0)
    def _():
        o_ref[...] += prod


def value_own(core, x, w):
    tok, _ = x.shape
    rows, cols = w.shape
    steps = rows // 512
    return pl.pallas_call(
        value_own_kernel,
        out_shape=sds((tok, cols), F32),
        grid_spec=pltpu.PrefetchScalarGridSpec(
            num_scalar_prefetch=1,
            grid=(steps,),
            in_specs=[
                pl.BlockSpec((tok, 512), lambda s, core: (0, core[0] * steps + s)),
                pl.BlockSpec((512, cols), lambda s, core: (s, 0)),
            ],
            out_specs=pl.BlockSpec((tok, cols), lambda s, core: (0, 0)),
        ),
        compiler_params=params(),
        cost_estimate=cost(2 * tok * rows * cols, 2 * (tok * rows + rows * cols)),
        name="value_own",
    )(core, x, w)


def value_rest_kernel(core, x_ref, w_ref, part_ref, k_ref, v_ref, pair_ref, acc):
    step = pl.program_id(0)
    prod = dot(x_ref[...], w_ref[...])

    @pl.when(step == 0)
    def _():
        acc[...] = part_ref[...] + prod

    @pl.when(step > 0)
    def _():
        acc[...] += prod

    @pl.when(step == pl.num_programs(0) - 1)
    def _():
        v = acc[...].astype(BF16)
        v_ref[...] = v
        for h in range(v.shape[1] // HDIM):
            cols = slice(h * HDIM, (h + 1) * HDIM)
            pair_ref[cols, :] = dot(k_ref[:, cols], v[:, cols], TN).astype(BF16)


def value_rest(core, x, w, part, k):
    tok, _ = x.shape
    rows, cols = w.shape
    steps = rows // 512
    return pl.pallas_call(
        value_rest_kernel,
        out_shape=(sds((tok, cols), BF16), sds((cols, HDIM), BF16)),
        grid_spec=pltpu.PrefetchScalarGridSpec(
            num_scalar_prefetch=1,
            grid=(steps,),
            in_specs=[
                pl.BlockSpec((tok, 512), lambda s, core: (0, (1 - core[0]) * steps + s)),
                pl.BlockSpec((512, cols), lambda s, core: (s, 0)),
                pl.BlockSpec((tok, cols), lambda s, core: (0, 0)),
                pl.BlockSpec((tok, cols), lambda s, core: (0, 0)),
            ],
            out_specs=(
                pl.BlockSpec((tok, cols), lambda s, core: (0, 0)),
                pl.BlockSpec((cols, HDIM), lambda s, core: (0, 0)),
            ),
            scratch_shapes=[pltpu.VMEM((tok, cols), F32)],
        ),
        compiler_params=params(),
        cost_estimate=cost(2 * tok * rows * cols, 2 * (tok * rows + rows * cols)),
        name="value_rest",
    )(core, x, w, part, k)


def tril(scores):
    rows = lax.broadcasted_iota(jnp.int32, scores.shape, 0)
    cols = lax.broadcasted_iota(jnp.int32, scores.shape, 1)
    return jnp.where(rows >= cols, scores, 0.0).astype(BF16)


def head_spec(tok):
    return pl.BlockSpec((tok, HDIM), lambda h: (0, h))


def state_spec():
    return pl.BlockSpec((HDIM, HDIM), lambda h: (h, 0))


def mask_spec(tok):
    return pl.BlockSpec((1, tok, tok), lambda h: (h, 0, 0))


def inside_kernel(q_ref, k_ref, v_ref, m_ref, a_ref):
    m = tril(dot(q_ref[...], k_ref[...], NT))
    m_ref[0] = m
    a_ref[...] = dot(m, v_ref[...])


def inside(q, k, v):
    tok, cols = q.shape
    heads = cols // HDIM
    return pl.pallas_call(
        inside_kernel,
        out_shape=(sds((heads, tok, tok), BF16), sds((tok, cols), F32)),
        grid=(heads,),
        in_specs=[head_spec(tok)] * 3,
        out_specs=(mask_spec(tok), head_spec(tok)),
        compiler_params=params(),
        cost_estimate=cost(4 * tok * tok * cols, 10 * tok * cols + 2 * heads * tok * tok),
        name="inside",
    )(q, k, v)


def norm_kernel(q_ref, g_ref, a_ref, near_ref, far_ref, low_ref, state_ref, local_ref):
    state = (near_ref[...] + far_ref[...].astype(F32)).astype(BF16)
    state_ref[...] = state
    att = a_ref[...] + dot(q_ref[...], state)
    inv = lax.rsqrt(jnp.mean(att * att, axis=-1, keepdims=True) + 1e-05)
    normed = att * inv
    g = g_ref[...].astype(F32)
    low = (inv * (g - normed * jnp.mean(g * normed, axis=-1, keepdims=True))).astype(BF16)
    low_ref[...] = low
    local_ref[...] = dot(q_ref[...], low, TN).astype(BF16)


def norm_step(q, g, a, near, far):
    tok, cols = q.shape
    heads = cols // HDIM
    return pl.pallas_call(
        norm_kernel,
        out_shape=(sds((tok, cols), BF16), sds((cols, HDIM), BF16), sds((cols, HDIM), BF16)),
        grid=(heads,),
        in_specs=[head_spec(tok)] * 3 + [state_spec()] * 2,
        out_specs=(head_spec(tok), state_spec(), state_spec()),
        compiler_params=params(),
        cost_estimate=cost(4 * tok * cols * HDIM, 10 * tok * cols),
        name="norm_grad",
    )(q, g, a, near, far)


def cross_kernel(q_ref, k_ref, v_ref, low_ref, m_ref, state_ref, qg_ref, kp_ref, vp_ref):
    low = low_ref[...]
    c = tril(dot(low, v_ref[...], NT))
    qg_ref[...] = (dot(c, k_ref[...]) + dot(low, state_ref[...], NT)).astype(BF16)
    kp_ref[...] = dot(c, q_ref[...], TN)
    vp_ref[...] = dot(m_ref[0], low, TN)


def cross_step(q, k, v, low, m, state):
    tok, cols = q.shape
    heads = cols // HDIM
    return pl.pallas_call(
        cross_kernel,
        out_shape=(sds((tok, cols), BF16), sds((tok, cols), F32), sds((tok, cols), F32)),
        grid=(heads,),
        in_specs=[head_spec(tok)] * 4 + [mask_spec(tok), state_spec()],
        out_specs=(head_spec(tok),) * 3,
        compiler_params=params(),
        cost_estimate=cost(8 * tok * tok * cols, 18 * tok * cols + 2 * heads * tok * tok),
        name="cross",
    )(q, k, v, low, m, state)


def value_grad_kernel(core, k_ref, vp_ref, near_ref, far_ref, own_ref, other_ref, vg_ref, state_ref, out_ref):
    step = pl.program_id(0)
    half = pl.num_programs(0) // 2

    @pl.when(step == 0)
    def _():
        for h in range(k_ref.shape[1] // HDIM):
            cols = slice(h * HDIM, (h + 1) * HDIM)
            state = (near_ref[cols, :] + far_ref[cols, :].astype(F32)).astype(BF16)
            state_ref[cols, :] = state
            vg_ref[:, cols] = (vp_ref[:, cols] + dot(k_ref[:, cols], state)).astype(BF16)

    @pl.when(step < half)
    def _():
        out_ref[...] = dot(vg_ref[...], own_ref[...], NT).astype(BF16)

    @pl.when(step >= half)
    def _():
        out_ref[...] = dot(vg_ref[...], other_ref[...], NT).astype(BF16)


def value_grad_step(core, k, vp, near, far, w_own, w_other):
    tok, cols = k.shape
    rows = w_own.shape[0]
    half = rows // 512
    whole = pl.BlockSpec((tok, cols), lambda s, core: (0, 0))
    states = pl.BlockSpec((cols, HDIM), lambda s, core: (0, 0))
    return pl.pallas_call(
        value_grad_kernel,
        out_shape=(sds((tok, cols), BF16), sds((cols, HDIM), BF16), sds((tok, 2 * rows), BF16)),
        grid_spec=pltpu.PrefetchScalarGridSpec(
            num_scalar_prefetch=1,
            grid=(2 * half,),
            in_specs=[
                whole,
                whole,
                states,
                states,
                pl.BlockSpec((512, cols), lambda s, core: (jnp.minimum(s, half - 1), 0)),
                pl.BlockSpec((512, cols), lambda s, core: (jnp.maximum(s - half, 0), 0)),
            ],
            out_specs=(
                whole,
                states,
                pl.BlockSpec(
                    (tok, 512), lambda s, core: (0, lax.rem(s + core[0] * half, 2 * half))
                ),
            ),
        ),
        compiler_params=params(),
        cost_estimate=cost(4 * tok * rows * cols, 4 * tok * rows + 4 * rows * cols),
        name="value_grad",
    )(core, k, vp, near, far, w_own, w_other)


def key_grad_kernel(v_ref, kp_ref, state_ref, kg_ref):
    kg_ref[...] = (kp_ref[...] + dot(v_ref[...], state_ref[...], NT)).astype(BF16)


def key_grad_step(v, kp, state):
    tok, cols = v.shape
    return pl.pallas_call(
        key_grad_kernel,
        out_shape=sds((tok, cols), BF16),
        grid=(cols // HDIM,),
        in_specs=[head_spec(tok), head_spec(tok), state_spec()],
        out_specs=head_spec(tok),
        compiler_params=params(),
        cost_estimate=cost(2 * tok * cols * HDIM, 8 * tok * cols),
        name="key_grad",
    )(v, kp, state)


def weight_grad_kernel(scale, core, vg_ref, x_ref, mine_ref, other_ref, turned):
    @pl.when(pl.program_id(0) == 0)
    def _():
        turned[...] = vg_ref[...].T

    res = dot(turned[...], x_ref[...]) * scale
    first = core[0] == 0
    for p in range(x_ref.shape[1] // 256):
        a = res[:, p * 256 : p * 256 + 128]
        b = res[:, p * 256 + 128 : p * 256 + 256]
        mine_ref[p] = jnp.where(first, a, b).astype(BF16)
        other_ref[p] = jnp.where(first, b, a).astype(BF16)


def weight_grad_step(core, vg, x, scale):
    tok, cols = vg.shape
    width = x.shape[1]
    pieces = width // 256
    out = pl.BlockSpec((2, cols, 128), lambda s, core: (s, 0, 0))

    def body(*refs):
        weight_grad_kernel(scale, *refs)

    return pl.pallas_call(
        body,
        out_shape=(sds((pieces, cols, 128), BF16),) * 2,
        grid_spec=pltpu.PrefetchScalarGridSpec(
            num_scalar_prefetch=1,
            grid=(width // 512,),
            in_specs=[
                pl.BlockSpec((tok, cols), lambda s, core: (0, 0)),
                pl.BlockSpec((tok, 512), lambda s, core: (0, s)),
            ],
            out_specs=(out, out),
            scratch_shapes=[pltpu.VMEM((cols, tok), BF16)],
        ),
        compiler_params=params(),
        cost_estimate=cost(2 * tok * width * cols, 2 * tok * width + 2 * width * cols),
        name="weight_grad",
    )(core, vg, x)


SIDE = 4


def along_x(a, k):
    return lax.ppermute(
        a, "ctx", [(i, i + SIDE * k) for i in range(16) if 0 <= i + SIDE * k < 16]
    )


def along_x_ring(a, k):
    return lax.ppermute(a, "ctx", [(i, (i + SIDE * k) % 16) for i in range(16)])


def along_y_ring(a, k):
    return lax.ppermute(
        a, "ctx", [(i, i // SIDE * SIDE + (i + k) % SIDE) for i in range(16)]
    )


def swap(a):
    return lax.ppermute(a, "fsdp", [(0, 1), (1, 0)])


def total(*terms):
    return sum(t.astype(F32) for t in terms)


def exclusive(mine, y, core, sign):
    got = [along_x(mine, sign * k) for k in (1, 2, 3)]
    before = total(*got)
    both = (before + mine.astype(F32)).astype(BF16)
    alone = before.astype(BF16)
    got = []
    for k in (1, 2, 3):
        onward = (y + k < SIDE) if sign == 1 else (y - k >= 0)
        got.append(along_y_ring(jnp.where(onward, both, alone), sign * k))
    near = before + total(*got)
    ahead = (core == 0) if sign == 1 else (core == 1)
    far = swap(jnp.where(ahead, near + mine.astype(F32), near).astype(BF16))
    return near, far


def pick(a, place):
    return lax.dynamic_index_in_dim(a, lax.rem(place, SIDE), 0, False)


def local(layer_input, query_act, key_act, out_grad, value_weight):
    tok = layer_input.shape[0]
    core = lax.axis_index("fsdp")
    place = lax.axis_index("ctx")
    x, y = place // SIDE, lax.rem(place, SIDE)
    core_arr = core.reshape(1).astype(jnp.int32)

    weight_other = swap(value_weight)
    part = value_own(core_arr, layer_input, value_weight)
    value, pair = value_rest(core_arr, layer_input, weight_other, part, key_act)
    masked, attended = inside(query_act, key_act, value)
    near, far = exclusive(pair, y, core, 1)
    low, state, own_grad = norm_step(query_act, out_grad, attended, near, far)
    query_grad, key_part, value_part = cross_step(query_act, key_act, value, low, masked, state)
    near_g, far_g = exclusive(own_grad, y, core, -1)
    value_grad, state_grad, partial_input = value_grad_step(
        core_arr, key_act, value_part, near_g, far_g, value_weight, weight_other
    )
    input_grad = lax.psum_scatter(partial_input, "head", scatter_dimension=1, tiled=True)

    seq_devices = lax.axis_size(("ctx", "fsdp"))
    scale = 1.0 / math.sqrt(tok * seq_devices)
    mine, other = weight_grad_step(core_arr, value_grad, layer_input, scale)
    key_grad = key_grad_step(value, key_part, state_grad)
    chip = total(mine, swap(other)).astype(BF16).reshape((SIDE, SIDE) + mine.shape[1:])
    got = [along_x_ring(pick(chip, x + k), k) for k in (1, 2, 3)]
    line = total(pick(chip, x), *got).astype(BF16)
    got = [along_y_ring(pick(line, y + k), k) for k in (1, 2, 3)]
    weight_grad = total(pick(line, y), *got).T
    return (query_grad, key_grad, input_grad, weight_grad)


def solution(mesh):
    in_specs = (
        P(("ctx", "fsdp"), None),
        P(("ctx", "fsdp"), "head"),
        P(("ctx", "fsdp"), "head"),
        P(("ctx", "fsdp"), "head"),
        P("fsdp", "head"),
    )
    out_specs = (
        P(("ctx", "fsdp"), "head"),
        P(("ctx", "fsdp"), "head"),
        P(("ctx", "fsdp"), "head"),
        P(("ctx", "fsdp"), "head"),
    )
    return jax.shard_map(local, mesh=mesh, in_specs=in_specs, out_specs=out_specs, check_vma=False)
```

time: 373 us -> 154 us (0.41)
  waiting for transfers between devices: 277 us -> 56.5 us
  matrix products: 32.4 us -> 0 us
  starting transfers between devices: 0.38 us -> 30.7 us
  Pallas kernels: 0 us -> 26.3 us
  other arithmetic: 30.5 us -> 4.91 us
    all_gather x3 -> x0, waiting for transfers between devices: 144 us -> none  [the longest x1 71.2 us: entering_2(): lax.all_gather(array.astype(jnp.bfloat16 if array.dtype == jnp.float32 el...]
    unnamed x6 -> x1, waiting for transfers between devices: 77.5 us -> 0.02 us
    ppermute x0 -> x22, waiting for transfers between devices: none -> 56.2 us  [the longest x3 22.4 us: along_x_ring(): return lax.ppermute(a, 'ctx', [(i, (i + SIDE * k) % 16) for i in range(16)])]
    reduce_scatter x1, waiting for transfers between devices: 56.4 us -> 0.26 us  [local(): lax.psum_scatter(partial_input, 'head', scatter_dimension=1, tiled=True)]
    dot_general x15 -> x0, matrix products: 32.4 us -> none  [the longest x7 8.56 us: lowdot(): jnp.einsum(pattern, former, latter, preferred_element_type=jnp.float32)]
    ppermute x0 -> x22, starting transfers between devices: none -> 30.6 us  [the longest x6 12.7 us: along_x(): lax.ppermute(a, 'ctx', [(i, i + SIDE * k) for i in range(16) if 0 <= i +...]
    add x31 -> x0, other arithmetic: 29.9 us -> none  [add_states(): return earlier + following]
    pallas_call x0 -> x8, Pallas kernels: none -> 26.3 us  [the longest x1 5.47 us: weight_grad_step(): pl.pallas_call(body, out_shape=(sds((pieces, cols, 128), BF16),) * 2, gri...]
  transfers between devices with their start and end apart: 5 -> 23, of which waited for: 5 -> 15; matrix products, arithmetic and copies ran while one was open for 6% -> 5% of each run, Pallas kernels for 0% -> 11%
where the time goes in v1:
time: 154 us; the launch traced here: 151 us
  waiting for transfers between devices  56.5 us (37%)
  starting transfers between devices  30.7 us (20%)
  Pallas kernels  26.3 us (17%)
  local copies, waits for them, and re-layouts  18.3 us (12%)
  between operations  14.4 us (9%)
  other arithmetic  4.91 us (3%)
    ppermute x3, waiting for transfers between devices, along_x_ring(): return lax.ppermute(a, 'ctx', [(i, (i + SIDE * k) % 16) for i in range(16)])  22.4 us
    ppermute x9, waiting for transfers between devices, along_y_ring(): lax.ppermute(a, 'ctx', [(i, i // SIDE * SIDE + (i + k) % SIDE) for i in r...  18.4 us
    unnamed x31, local copies, waits for them, and re-layouts  15 us
    ppermute x6, starting transfers between devices, along_x(): lax.ppermute(a, 'ctx', [(i, i + SIDE * k) for i in range(16) if 0 <= i +...  12.7 us
    ppermute x6, waiting for transfers between devices, along_x(): lax.ppermute(a, 'ctx', [(i, i + SIDE * k) for i in range(16) if 0 <= i +...  11.3 us
    ppermute x9, starting transfers between devices, along_y_ring(): lax.ppermute(a, 'ctx', [(i, i // SIDE * SIDE + (i + k) % SIDE) for i in r...  11 us
    ppermute x3, starting transfers between devices, along_x_ring(): return lax.ppermute(a, 'ctx', [(i, (i + SIDE * k) % 16) for i in range(16)])  6.13 us
    pallas_call x1, Pallas kernels, weight_grad_step(): pl.pallas_call(body, out_shape=(sds((pieces, cols, 128), BF16),) * 2, gri...  5.47 us
  transfers between devices with their start and end apart: 23, of which 15 were waited for; matrix products, arithmetic and copies ran while one was open for 5% of the time, Pallas kernels for 11%

profile of v1, /device:TPU:24, one launch (start us, length us, event | category | flops | bytes accessed | tf_op | source)
XLA Modules:
  0.0 151.0 jit_solution(15720799213333085083)
XLA Ops:
  7.3 2.2 %copy-done = bf16[512,4096]{1,0:T(8,128)(2,1)S(1)} copy-done((bf16[512,4096]{1,0:T(8,128)(2,1)S(1)}, bf16[512,4096]{1,0:T(8,128)(2,1)}, u32[]{:S(2)}) %copy-start) | copy-done | bytes 4194328
  11.1 2.3 %value_own.1.part_ref = f32[512,512]{1,0:T(8,128)S(1)} custom-call(s32[1]{0:T(128)} %bitcast.core.refs_0_, bf16[512,4096]{1,0:T(8,128)(2,1)S(1)} %copy-done, bf16[2048,512]{1,0:T(8,128)(2,1)S(1)} %copy-done.7), custom_call_target="tpu_custom_call" | custom-call | flops 1073741824 | bytes 4194304 | tf_op jit(solution)/shard_map/value_own/pallas_call | solution.py:50
  16.4 2.8 %value_rest.1 = (bf16[512,512]{1,0:T(8,128)(2,1)S(1)}, bf16[512,128]{1,0:T(8,128)(2,1)S(1)}) custom-call(s32[1]{0:T(128)} %bitcast.core.refs_0_, bf16[512,4096]{1,0:T(8,128)(2,1)S(1)} %copy-done, bf16[2048,512]{1,0:T(8,128)(2,1)S(1)} %copy-done.10, f32[512,512]{1,0:T(8,128)S(1)} %value_own.1.part_ref, bf16[512,512]{1,0:T(8,128)(2,1)S(1)} %copy-done.4), custom_call_target="tpu_custom_call" | custom-call | flops 1073741824 | bytes 4194304 | tf_op jit(solution)/shard_map/value_rest/pallas_call | solution.py:93
  19.2 4.8 %collective-permute-start.3 = (bf16[512,128]{1,0:T(8,128)(2,1)S(1)}, bf16[512,128]{1,0:T(8,128)(2,1)S(1)}, u32[]{:S(2)}, u32[]{:S(2)}) collective-permute-start(bf16[512,128]{1,0:T(8,128)(2,1)S(1)} %get-tuple-element.21), channel_id=1, source_target_pairs={{0,192},{16,208},{32,224},{48,240},{1,193},{17,209},{33,225},{49,2... | collective-permute-start | bytes 393224 | tf_op jit(solution)/shard_map/ppermute | solution.py:325
  25.3 2.8 %collective-permute-start.1 = (bf16[512,128]{1,0:T(8,128)(2,1)S(1)}, bf16[512,128]{1,0:T(8,128)(2,1)S(1)}, u32[]{:S(2)}, u32[]{:S(2)}) collective-permute-start(bf16[512,128]{1,0:T(8,128)(2,1)S(1)} %get-tuple-element.21), channel_id=1, source_target_pairs={{0,64},{16,80},{32,96},{48,112},{64,128},{80,144},{96,160},{112,17... | collective-permute-start | bytes 393224 | tf_op jit(solution)/shard_map/ppermute | solution.py:325
  33.4 2.2 %collective-permute-start.4 = (bf16[512,128]{1,0:T(8,128)(2,1)S(1)}, bf16[512,128]{1,0:T(8,128)(2,1)S(1)}, u32[]{:S(2)}, u32[]{:S(2)}) collective-permute-start(bf16[512,128]{1,0:T(8,128)(2,1)S(1)} %get-tuple-element.41), channel_id=1, source_target_pairs={{0,16},{16,32},{32,48},{48,0},{64,80},{80,96},{96,112},{112,64},{1... | collective-permute-start | bytes 393224 | tf_op jit(solution)/shard_map/ppermute | solution.py:335
  35.6 5.3 %collective-permute-done.6 = bf16[512,128]{1,0:T(8,128)(2,1)S(1)} collective-permute-done((bf16[512,128]{1,0:T(8,128)(2,1)S(1)}, bf16[512,128]{1,0:T(8,128)(2,1)S(1)}, u32[]{:S(2)}, u32[]{:S(2)}) %collective-permute-start.6) | collective-permute-done | bytes 131104 | tf_op jit(solution)/shard_map/ppermute | solution.py:335
  41.6 2.5 %inside.1 = (bf16[4,512,512]{2,1,0:T(8,128)(2,1)S(1)}, f32[512,512]{1,0:T(8,128)S(1)}) custom-call(bf16[512,512]{1,0:T(8,128)(2,1)S(1)} %copy-done.3, bf16[512,512]{1,0:T(8,128)(2,1)S(1)} %copy-done.4, bf16[512,512]{1,0:T(8,128)(2,1)S(1)} %get-tuple-element.19.v_ref), custom_call_target="tpu_custom_call" | custom-call | flops 536870912 | bytes 4718592 | tf_op jit(solution)/shard_map/inside/pallas_call | solution.py:144
  45.5 2.5 %norm_grad.1 = (bf16[512,512]{1,0:T(8,128)(2,1)S(1)}, bf16[512,128]{1,0:T(8,128)(2,1)S(1)}, bf16[512,128]{1,0:T(8,128)(2,1)S(1)}) custom-call(bf16[512,512]{1,0:T(8,128)(2,1)S(1)} %copy-done.3, bf16[512,512]{1,0:T(8,128)(2,1)S(1)} %copy-done.14, f32[512,512]{1,0:T(8,128)S(1)} %get-tuple-element.20.a_ref, f32[512,128]{1,0:T(8,128)S(1)} %get-tuple-element.40.near_ref, ...), custom_call_target="tpu_custom_call" | custom-call | flops 134217728 | bytes 2621440 | tf_op jit(solution)/shard_map/norm_grad/pallas_call | solution.py:171
  52.0 7.9 %collective-permute-done.10 = bf16[512,128]{1,0:T(8,128)(2,1)S(1)} collective-permute-done((bf16[512,128]{1,0:T(8,128)(2,1)S(1)}, bf16[512,128]{1,0:T(8,128)(2,1)S(1)}, u32[]{:S(2)}, u32[]{:S(2)}) %collective-permute-start.10) | collective-permute-done | bytes 131104 | tf_op jit(solution)/shard_map/ppermute | solution.py:325
  60.0 2.8 %collective-permute-start.13 = (bf16[512,128]{1,0:T(8,128)(2,1)S(1)}, bf16[512,128]{1,0:T(8,128)(2,1)S(1)}, u32[]{:S(2)}, u32[]{:S(2)}) collective-permute-start(bf16[512,128]{1,0:T(8,128)(2,1)S(1)} %get-tuple-element.52), channel_id=1, source_target_pairs={{0,16},{16,32},{32,48},{48,0},{64,80},{80,96},{96,112},{112,64},{1... | collective-permute-start | bytes 393224 | tf_op jit(solution)/shard_map/ppermute | solution.py:335
  63.7 4.5 %collective-permute-done.13 = bf16[512,128]{1,0:T(8,128)(2,1)S(1)} collective-permute-done((bf16[512,128]{1,0:T(8,128)(2,1)S(1)}, bf16[512,128]{1,0:T(8,128)(2,1)S(1)}, u32[]{:S(2)}, u32[]{:S(2)}) %collective-permute-start.13) | collective-permute-done | bytes 131104 | tf_op jit(solution)/shard_map/ppermute | solution.py:335
  68.2 2.3 %collective-permute-done.12 = bf16[512,128]{1,0:T(8,128)(2,1)S(1)} collective-permute-done((bf16[512,128]{1,0:T(8,128)(2,1)S(1)}, bf16[512,128]{1,0:T(8,128)(2,1)S(1)}, u32[]{:S(2)}, u32[]{:S(2)}) %collective-permute-start.12) | collective-permute-done | bytes 131104 | tf_op jit(solution)/shard_map/ppermute | solution.py:335
  73.4 3.9 %cross.1 = (bf16[512,512]{1,0:T(8,128)(2,1)}, f32[512,512]{1,0:T(8,128)S(1)}, f32[512,512]{1,0:T(8,128)S(1)}) custom-call(bf16[512,512]{1,0:T(8,128)(2,1)S(1)} %copy-done.3, bf16[512,512]{1,0:T(8,128)(2,1)S(1)} %copy-done.4, bf16[512,512]{1,0:T(8,128)(2,1)S(1)} %get-tuple-element.19.v_ref, bf16[512,512]{1,0:T(8,128)(2,1)S(1)} %get-tuple-element.22.low_ref, ...), custom_call_target="tpu_custom_call" | custom-call | flops 1073741824 | bytes 6815744 | tf_op jit(solution)/shard_map/cross/pallas_call | solution.py:194
  78.3 4.6 %value_grad.1 = (bf16[512,512]{1,0:T(8,128)(2,1)S(1)}, bf16[512,128]{1,0:T(8,128)(2,1)S(1)}, bf16[512,4096]{1,0:T(8,128)(2,1)S(1)}) custom-call(s32[1]{0:T(128)} %bitcast.core.refs_0_, bf16[512,512]{1,0:T(8,128)(2,1)S(1)} %copy-done.4, f32[512,512]{1,0:T(8,128)S(1)} %get-tuple-element.27.vp_ref, f32[512,128]{1,0:T(8,128)S(1)} %get-tuple-element.35.near_ref, ...), custom_call_target="tpu_custom_call" | custom-call | flops 2147483648 | bytes 8388608 | tf_op jit(solution)/shard_map/value_grad/pallas_call | solution.py:233
  87.1 5.5 %weight_grad.1 = (bf16[16,512,128]{2,1,0:T(8,128)(2,1)S(1)}, bf16[16,512,128]{2,1,0:T(8,128)(2,1)}) custom-call(s32[1]{0:T(128)} %bitcast.core.refs_0_, bf16[512,512]{1,0:T(8,128)(2,1)S(1)} %get-tuple-element.31.refs_1_, bf16[512,4096]{1,0:T(8,128)(2,1)S(1)} %copy-done.1), custom_call_target="tpu_custom_call" | custom-call | flops 2147483648 | bytes 8388608 | tf_op jit(solution)/shard_map/weight_grad/pallas_call | solution.py:302
  93.1 4.1 %collective-permute-done.15 = bf16[16,512,128]{2,1,0:T(8,128)(2,1)} collective-permute-done((bf16[16,512,128]{2,1,0:T(8,128)(2,1)}, bf16[16,512,128]{2,1,0:T(8,128)(2,1)}, u32[]{:S(2)}, u32[]{:S(2)}) %collective-permute-start.15) | collective-permute-done | bytes 2097184 | tf_op jit(solution)/shard_map/ppermute | solution.py:341
  100.6 2.2 %collective-permute-start.18 = (bf16[4,512,128]{1,2,0:T(8,128)(2,1)}, bf16[4,512,128]{1,2,0:T(8,128)(2,1)S(1)}, u32[]{:S(2)}, u32[]{:S(2)}) collective-permute-start(bf16[4,512,128]{1,2,0:T(8,128)(2,1)} %bitcast.5), channel_id=1, source_target_pairs={{0,192},{16,208},{32,224},{48,240},{64,0},{80,16},{96,32},{112,48}... | collective-permute-start | bytes 1572872 | tf_op jit(solution)/shard_map/ppermute | solution.py:331
  103.8 3.9 %collective-permute-start.17 = (bf16[4,512,128]{1,2,0:T(8,128)(2,1)}, bf16[4,512,128]{1,2,0:T(8,128)(2,1)}, u32[]{:S(2)}, u32[]{:S(2)}) collective-permute-start(bf16[4,512,128]{1,2,0:T(8,128)(2,1)} %bitcast.4), channel_id=1, source_target_pairs={{0,128},{16,144},{32,160},{48,176},{64,192},{80,208},{96,224},{112... | collective-permute-start | bytes 1572872 | tf_op jit(solution)/shard_map/ppermute | solution.py:331
  109.0 8.5 %collective-permute-done.18 = bf16[4,512,128]{1,2,0:T(8,128)(2,1)S(1)} collective-permute-done((bf16[4,512,128]{1,2,0:T(8,128)(2,1)}, bf16[4,512,128]{1,2,0:T(8,128)(2,1)S(1)}, u32[]{:S(2)}, u32[]{:S(2)}) %collective-permute-start.18) | collective-permute-done | bytes 524320 | tf_op jit(solution)/shard_map/ppermute | solution.py:331
  117.5 3.3 %collective-permute-done.17 = bf16[4,512,128]{1,2,0:T(8,128)(2,1)} collective-permute-done((bf16[4,512,128]{1,2,0:T(8,128)(2,1)}, bf16[4,512,128]{1,2,0:T(8,128)(2,1)}, u32[]{:S(2)}, u32[]{:S(2)}) %collective-permute-start.17) | collective-permute-done | bytes 524320 | tf_op jit(solution)/shard_map/ppermute | solution.py:331
  120.9 10.6 %collective-permute-done.16 = bf16[4,512,128]{1,2,0:T(8,128)(2,1)} collective-permute-done((bf16[4,512,128]{1,2,0:T(8,128)(2,1)}, bf16[4,512,128]{1,2,0:T(8,128)(2,1)}, u32[]{:S(2)}, u32[]{:S(2)}) %collective-permute-start.16) | collective-permute-done | bytes 524320 | tf_op jit(solution)/shard_map/ppermute | solution.py:331
  133.1 2.2 %collective-permute-start.20 = (bf16[512,128]{0,1:T(8,128)(2,1)S(1)}, bf16[512,128]{0,1:T(8,128)(2,1)S(1)}, u32[]{:S(2)}, u32[]{:S(2)}) collective-permute-start(bf16[512,128]{0,1:T(8,128)(2,1)S(1)} %get-tuple-element.50), channel_id=1, source_target_pairs={{0,32},{16,48},{32,0},{48,16},{64,96},{80,112},{96,64},{112,80},{1... | collective-permute-start | bytes 393224 | tf_op jit(solution)/shard_map/ppermute | solution.py:335
  138.4 4.1 %collective-permute-done.21 = bf16[512,128]{0,1:T(8,128)(2,1)S(1)} collective-permute-done((bf16[512,128]{0,1:T(8,128)(2,1)S(1)}, bf16[512,128]{0,1:T(8,128)(2,1)S(1)}, u32[]{:S(2)}, u32[]{:S(2)}) %collective-permute-start.21) | collective-permute-done | bytes 131104 | tf_op jit(solution)/shard_map/ppermute | solution.py:335
  (76 shorter events, 38.9 us)
Async XLA Ops:
  7.2 137.0 %reduce-scatter.2.cloned.1.call-start = ((), (), s32[]{:S(2)}) async-start(), calls=%async_computation.1 | async-start | bytes 4718592 | tf_op jit(solution)/shard_map/reduce_scatter | solution.py:385
  7.2 6.2 %collective-permute-start = (bf16[2048,512]{1,0:T(8,128)(2,1)}, bf16[2048,512]{1,0:T(8,128)(2,1)S(1)}, u32[]{:S(2)}, u32[]{:S(2)}) collective-permute-start(bf16[2048,512]{1,0:T(8,128)(2,1)} %own_ref.1), channel_id=1, source_target_pairs={{0,1},{1,0},{2,3},{3,2},{4,5},{5,4},{6,7},{7,6},{8,9},{9,8},{10,11... | collective-permute-start | bytes 6291464 | tf_op jit(solution)/shard_map/ppermute | solution.py:341
  19.2 11.0 %collective-permute-start.3 = (bf16[512,128]{1,0:T(8,128)(2,1)S(1)}, bf16[512,128]{1,0:T(8,128)(2,1)S(1)}, u32[]{:S(2)}, u32[]{:S(2)}) collective-permute-start(bf16[512,128]{1,0:T(8,128)(2,1)S(1)} %get-tuple-element.21), channel_id=1, source_target_pairs={{0,192},{16,208},{32,224},{48,240},{1,193},{17,209},{33,225},{49,2... | collective-permute-start | bytes 393224 | tf_op jit(solution)/shard_map/ppermute | solution.py:325
  24.0 6.2 %collective-permute-start.2 = (bf16[512,128]{1,0:T(8,128)(2,1)S(1)}, bf16[512,128]{1,0:T(8,128)(2,1)S(1)}, u32[]{:S(2)}, u32[]{:S(2)}) collective-permute-start(bf16[512,128]{1,0:T(8,128)(2,1)S(1)} %get-tuple-element.21), channel_id=1, source_target_pairs={{0,128},{16,144},{32,160},{48,176},{64,192},{80,208},{96,224},{112... | collective-permute-start | bytes 393224 | tf_op jit(solution)/shard_map/ppermute | solution.py:325
  25.3 6.2 %collective-permute-start.1 = (bf16[512,128]{1,0:T(8,128)(2,1)S(1)}, bf16[512,128]{1,0:T(8,128)(2,1)S(1)}, u32[]{:S(2)}, u32[]{:S(2)}) collective-permute-start(bf16[512,128]{1,0:T(8,128)(2,1)S(1)} %get-tuple-element.21), channel_id=1, source_target_pairs={{0,64},{16,80},{32,96},{48,112},{64,128},{80,144},{96,160},{112,17... | collective-permute-start | bytes 393224 | tf_op jit(solution)/shard_map/ppermute | solution.py:325
  31.6 9.2 %collective-permute-start.6 = (bf16[512,128]{1,0:T(8,128)(2,1)S(1)}, bf16[512,128]{1,0:T(8,128)(2,1)S(1)}, u32[]{:S(2)}, u32[]{:S(2)}) collective-permute-start(bf16[512,128]{1,0:T(8,128)(2,1)S(1)} %get-tuple-element.54), channel_id=1, source_target_pairs={{0,48},{16,0},{32,16},{48,32},{64,112},{80,64},{96,80},{112,96},{1... | collective-permute-start | bytes 393224 | tf_op jit(solution)/shard_map/ppermute | solution.py:335
  32.4 8.4 %collective-permute-start.5 = (bf16[512,128]{1,0:T(8,128)(2,1)S(1)}, bf16[512,128]{1,0:T(8,128)(2,1)S(1)}, u32[]{:S(2)}, u32[]{:S(2)}) collective-permute-start(bf16[512,128]{1,0:T(8,128)(2,1)S(1)} %get-tuple-element.53), channel_id=1, source_target_pairs={{0,32},{16,48},{32,0},{48,16},{64,96},{80,112},{96,64},{112,80},{1... | collective-permute-start | bytes 393224 | tf_op jit(solution)/shard_map/ppermute | solution.py:335
  33.4 8.0 %collective-permute-start.4 = (bf16[512,128]{1,0:T(8,128)(2,1)S(1)}, bf16[512,128]{1,0:T(8,128)(2,1)S(1)}, u32[]{:S(2)}, u32[]{:S(2)}) collective-permute-start(bf16[512,128]{1,0:T(8,128)(2,1)S(1)} %get-tuple-element.41), channel_id=1, source_target_pairs={{0,16},{16,32},{32,48},{48,0},{64,80},{80,96},{96,112},{112,64},{1... | collective-permute-start | bytes 393224 | tf_op jit(solution)/shard_map/ppermute | solution.py:335
  41.5 4.0 %collective-permute-start.7 = (bf16[512,128]{1,0:T(8,128)(2,1)S(1)}, bf16[512,128]{1,0:T(8,128)(2,1)S(1)}, u32[]{:S(2)}, u32[]{:S(2)}) collective-permute-start(bf16[512,128]{1,0:T(8,128)(2,1)S(1)} %get-tuple-element.39), channel_id=1, source_target_pairs={{0,1},{1,0},{2,3},{3,2},{4,5},{5,4},{6,7},{7,6},{8,9},{9,8},{10,11... | collective-permute-start | bytes 393224 | tf_op jit(solution)/shard_map/ppermute | solution.py:341
  48.1 11.8 %collective-permute-start.10 = (bf16[512,128]{1,0:T(8,128)(2,1)S(1)}, bf16[512,128]{1,0:T(8,128)(2,1)S(1)}, u32[]{:S(2)}, u32[]{:S(2)}) collective-permute-start(bf16[512,128]{1,0:T(8,128)(2,1)S(1)} %get-tuple-element.28), channel_id=1, source_target_pairs={{192,0},{208,16},{224,32},{240,48},{193,1},{209,17},{225,33},{241,... | collective-permute-start | bytes 393224 | tf_op jit(solution)/shard_map/ppermute | solution.py:325
  49.4 10.5 %collective-permute-start.9 = (bf16[512,128]{1,0:T(8,128)(2,1)S(1)}, bf16[512,128]{1,0:T(8,128)(2,1)S(1)}, u32[]{:S(2)}, u32[]{:S(2)}) collective-permute-start(bf16[512,128]{1,0:T(8,128)(2,1)S(1)} %get-tuple-element.28), channel_id=1, source_target_pairs={{128,0},{144,16},{160,32},{176,48},{192,64},{208,80},{224,96},{240... | collective-permute-start | bytes 393224 | tf_op jit(solution)/shard_map/ppermute | solution.py:325
  50.7 9.2 %collective-permute-start.8 = (bf16[512,128]{1,0:T(8,128)(2,1)S(1)}, bf16[512,128]{1,0:T(8,128)(2,1)S(1)}, u32[]{:S(2)}, u32[]{:S(2)}) collective-permute-start(bf16[512,128]{1,0:T(8,128)(2,1)S(1)} %get-tuple-element.28), channel_id=1, source_target_pairs={{64,0},{80,16},{96,32},{112,48},{128,64},{144,80},{160,96},{176,11... | collective-permute-start | bytes 393224 | tf_op jit(solution)/shard_map/ppermute | solution.py:325
  60.0 8.2 %collective-permute-start.13 = (bf16[512,128]{1,0:T(8,128)(2,1)S(1)}, bf16[512,128]{1,0:T(8,128)(2,1)S(1)}, u32[]{:S(2)}, u32[]{:S(2)}) collective-permute-start(bf16[512,128]{1,0:T(8,128)(2,1)S(1)} %get-tuple-element.52), channel_id=1, source_target_pairs={{0,16},{16,32},{32,48},{48,0},{64,80},{80,96},{96,112},{112,64},{1... | collective-permute-start | bytes 393224 | tf_op jit(solution)/shard_map/ppermute | solution.py:335
  62.8 7.8 %collective-permute-start.12 = (bf16[512,128]{1,0:T(8,128)(2,1)S(1)}, bf16[512,128]{1,0:T(8,128)(2,1)S(1)}, u32[]{:S(2)}, u32[]{:S(2)}) collective-permute-start(bf16[512,128]{1,0:T(8,128)(2,1)S(1)} %get-tuple-element.51), channel_id=1, source_target_pairs={{0,32},{16,48},{32,0},{48,16},{64,96},{80,112},{96,64},{112,80},{1... | collective-permute-start | bytes 393224 | tf_op jit(solution)/shard_map/ppermute | solution.py:335
  62.8 8.8 %collective-permute-start.11 = (bf16[512,128]{1,0:T(8,128)(2,1)S(1)}, bf16[512,128]{1,0:T(8,128)(2,1)S(1)}, u32[]{:S(2)}, u32[]{:S(2)}) collective-permute-start(bf16[512,128]{1,0:T(8,128)(2,1)S(1)} %get-tuple-element.36), channel_id=1, source_target_pairs={{0,48},{16,0},{32,16},{48,32},{64,112},{80,64},{96,80},{112,96},{1... | collective-permute-start | bytes 393224 | tf_op jit(solution)/shard_map/ppermute | solution.py:335
  71.7 6.6 %collective-permute-start.14 = (bf16[512,128]{1,0:T(8,128)(2,1)S(1)}, bf16[512,128]{1,0:T(8,128)(2,1)S(1)}, u32[]{:S(2)}, u32[]{:S(2)}) collective-permute-start(bf16[512,128]{1,0:T(8,128)(2,1)S(1)} %get-tuple-element.34), channel_id=1, source_target_pairs={{0,1},{1,0},{2,3},{3,2},{4,5},{5,4},{6,7},{7,6},{8,9},{9,8},{10,11... | collective-permute-start | bytes 393224 | tf_op jit(solution)/shard_map/ppermute | solution.py:341
  92.6 4.6 %collective-permute-start.15 = (bf16[16,512,128]{2,1,0:T(8,128)(2,1)}, bf16[16,512,128]{2,1,0:T(8,128)(2,1)}, u32[]{:S(2)}, u32[]{:S(2)}) collective-permute-start(bf16[16,512,128]{2,1,0:T(8,128)(2,1)} %get-tuple-element.33), channel_id=1, source_target_pairs={{0,1},{1,0},{2,3},{3,2},{4,5},{5,4},{6,7},{7,6},{8,9},{9,8},{10,11... | collective-permute-start | bytes 6291464 | tf_op jit(solution)/shard_map/ppermute | solution.py:341
  100.6 17.0 %collective-permute-start.18 = (bf16[4,512,128]{1,2,0:T(8,128)(2,1)}, bf16[4,512,128]{1,2,0:T(8,128)(2,1)S(1)}, u32[]{:S(2)}, u32[]{:S(2)}) collective-permute-start(bf16[4,512,128]{1,2,0:T(8,128)(2,1)} %bitcast.5), channel_id=1, source_target_pairs={{0,192},{16,208},{32,224},{48,240},{64,0},{80,16},{96,32},{112,48}... | collective-permute-start | bytes 1572872 | tf_op jit(solution)/shard_map/ppermute | solution.py:331
  103.8 17.0 %collective-permute-start.17 = (bf16[4,512,128]{1,2,0:T(8,128)(2,1)}, bf16[4,512,128]{1,2,0:T(8,128)(2,1)}, u32[]{:S(2)}, u32[]{:S(2)}) collective-permute-start(bf16[4,512,128]{1,2,0:T(8,128)(2,1)} %bitcast.4), channel_id=1, source_target_pairs={{0,128},{16,144},{32,160},{48,176},{64,192},{80,208},{96,224},{112... | collective-permute-start | bytes 1572872 | tf_op jit(solution)/shard_map/ppermute | solution.py:331
  108.8 22.6 %collective-permute-start.16 = (bf16[4,512,128]{1,2,0:T(8,128)(2,1)}, bf16[4,512,128]{1,2,0:T(8,128)(2,1)}, u32[]{:S(2)}, u32[]{:S(2)}) collective-permute-start(bf16[4,512,128]{1,2,0:T(8,128)(2,1)} %bitcast.3), channel_id=1, source_target_pairs={{0,64},{16,80},{32,96},{48,112},{64,128},{80,144},{96,160},{112,17... | collective-permute-start | bytes 1572872 | tf_op jit(solution)/shard_map/ppermute | solution.py:331
  108.8 27.5 %copy-start.13 = (f32[512,512]{1,0:T(8,128)S(1)}, f32[512,512]{1,0:T(8,128)}, u32[]{:S(2)}) copy-start(f32[512,512]{1,0:T(8,128)} %copy-done.12) | copy-start | bytes 3145732
  133.0 9.5 %collective-permute-start.21 = (bf16[512,128]{0,1:T(8,128)(2,1)S(1)}, bf16[512,128]{0,1:T(8,128)(2,1)S(1)}, u32[]{:S(2)}, u32[]{:S(2)}) collective-permute-start(bf16[512,128]{0,1:T(8,128)(2,1)S(1)} %get-tuple-element.49), channel_id=1, source_target_pairs={{0,48},{16,0},{32,16},{48,32},{64,112},{80,64},{96,80},{112,96},{1... | collective-permute-start | bytes 393224 | tf_op jit(solution)/shard_map/ppermute | solution.py:335
  133.1 9.4 %collective-permute-start.20 = (bf16[512,128]{0,1:T(8,128)(2,1)S(1)}, bf16[512,128]{0,1:T(8,128)(2,1)S(1)}, u32[]{:S(2)}, u32[]{:S(2)}) collective-permute-start(bf16[512,128]{0,1:T(8,128)(2,1)S(1)} %get-tuple-element.50), channel_id=1, source_target_pairs={{0,32},{16,48},{32,0},{48,16},{64,96},{80,112},{96,64},{112,80},{1... | collective-permute-start | bytes 393224 | tf_op jit(solution)/shard_map/ppermute | solution.py:335
  135.3 7.8 %collective-permute-start.19 = (bf16[512,128]{0,1:T(8,128)(2,1)S(1)}, bf16[512,128]{0,1:T(8,128)(2,1)S(1)}, u32[]{:S(2)}, u32[]{:S(2)}) collective-permute-start(bf16[512,128]{0,1:T(8,128)(2,1)S(1)} %get-tuple-element.48), channel_id=1, source_target_pairs={{0,16},{16,32},{32,48},{48,0},{64,80},{80,96},{96,112},{112,64},{1... | collective-permute-start | bytes 393224 | tf_op jit(solution)/shard_map/ppermute | solution.py:335
  (14 other events, 64.7 us)
Sparse Core Ops, SparseCore 0:
  85.1 59.0 reduce-scatter.1

commit v2 on v1

v2 whole, which is shorter than its diff:
```python
import math

import jax
import jax.numpy as jnp
from jax import lax
from jax.experimental import pallas as pl
from jax.experimental.pallas import tpu as pltpu
from jax.sharding import PartitionSpec as P

HDIM = 128
F32 = jnp.float32
BF16 = jnp.bfloat16
NT = (((1,), (1,)), ((), ()))
TN = (((0,), (0,)), ((), ()))
NN = (((1,), (0,)), ((), ()))


def dot(a, b, dims=NN):
    return lax.dot_general(a, b, dims, preferred_element_type=F32)


def params(**more):
    return pltpu.CompilerParams(vmem_limit_bytes=58 * 2**20, **more)


def cost(flops, nbytes):
    return pl.CostEstimate(flops=int(flops), bytes_accessed=int(nbytes), transcendentals=0)


def sds(shape, dtype):
    return jax.ShapeDtypeStruct(shape, dtype)


def value_own_kernel(core, x_ref, w_ref, o_ref):
    prod = dot(x_ref[...], w_ref[...])

    @pl.when(pl.program_id(0) == 0)
    def _():
        o_ref[...] = prod

    @pl.when(pl.program_id(0) > 0)
    def _():
        o_ref[...] += prod


def value_own(core, x, w):
    tok, _ = x.shape
    rows, cols = w.shape
    steps = rows // 512
    return pl.pallas_call(
        value_own_kernel,
        out_shape=sds((tok, cols), F32),
        grid_spec=pltpu.PrefetchScalarGridSpec(
            num_scalar_prefetch=1,
            grid=(steps,),
            in_specs=[
                pl.BlockSpec((tok, 512), lambda s, core: (0, core[0] * steps + s)),
                pl.BlockSpec((512, cols), lambda s, core: (s, 0)),
            ],
            out_specs=pl.BlockSpec((tok, cols), lambda s, core: (0, 0)),
        ),
        compiler_params=params(),
        cost_estimate=cost(2 * tok * rows * cols, 2 * (tok * rows + rows * cols)),
        name="value_own",
    )(core, x, w)


def value_rest_kernel(core, x_ref, w_ref, part_ref, k_ref, v_ref, pair_ref, acc):
    step = pl.program_id(0)
    prod = dot(x_ref[...], w_ref[...])

    @pl.when(step == 0)
    def _():
        acc[...] = part_ref[...] + prod

    @pl.when(step > 0)
    def _():
        acc[...] += prod

    @pl.when(step == pl.num_programs(0) - 1)
    def _():
        v = acc[...].astype(BF16)
        v_ref[...] = v
        for h in range(v.shape[1] // HDIM):
            cols = slice(h * HDIM, (h + 1) * HDIM)
            pair_ref[cols, :] = dot(k_ref[:, cols], v[:, cols], TN).astype(BF16)


def value_rest(core, x, w, part, k):
    tok, _ = x.shape
    rows, cols = w.shape
    steps = rows // 512
    return pl.pallas_call(
        value_rest_kernel,
        out_shape=(sds((tok, cols), BF16), sds((cols, HDIM), BF16)),
        grid_spec=pltpu.PrefetchScalarGridSpec(
            num_scalar_prefetch=1,
            grid=(steps,),
            in_specs=[
                pl.BlockSpec((tok, 512), lambda s, core: (0, (1 - core[0]) * steps + s)),
                pl.BlockSpec((512, cols), lambda s, core: (s, 0)),
                pl.BlockSpec((tok, cols), lambda s, core: (0, 0)),
                pl.BlockSpec((tok, cols), lambda s, core: (0, 0)),
            ],
            out_specs=(
                pl.BlockSpec((tok, cols), lambda s, core: (0, 0)),
                pl.BlockSpec((cols, HDIM), lambda s, core: (0, 0)),
            ),
            scratch_shapes=[pltpu.VMEM((tok, cols), F32)],
        ),
        compiler_params=params(),
        cost_estimate=cost(2 * tok * rows * cols, 2 * (tok * rows + rows * cols)),
        name="value_rest",
    )(core, x, w, part, k)


def tril(scores):
    rows = lax.broadcasted_iota(jnp.int32, scores.shape, 0)
    cols = lax.broadcasted_iota(jnp.int32, scores.shape, 1)
    return jnp.where(rows >= cols, scores, 0.0).astype(BF16)


def head_spec(tok):
    return pl.BlockSpec((tok, HDIM), lambda h: (0, h))


def state_spec():
    return pl.BlockSpec((HDIM, HDIM), lambda h: (h, 0))


ANY = pl.BlockSpec(memory_space=pl.ANY)


def inside_kernel(q_ref, k_ref, v_ref, a_ref):
    a_ref[...] = dot(tril(dot(q_ref[...], k_ref[...], NT)), v_ref[...])


def inside(q, k, v):
    tok, cols = q.shape
    return pl.pallas_call(
        inside_kernel,
        out_shape=sds((tok, cols), F32),
        grid=(cols // HDIM,),
        in_specs=[head_spec(tok)] * 3,
        out_specs=head_spec(tok),
        compiler_params=params(),
        cost_estimate=cost(4 * tok * tok * cols, 10 * tok * cols),
        name="inside",
    )(q, k, v)


def norm_kernel(q_ref, g_ref, a_ref, near_ref, far_ref, low_ref, state_ref, local_ref):
    state = (near_ref[...] + far_ref[...].astype(F32)).astype(BF16)
    state_ref[...] = state
    att = a_ref[...] + dot(q_ref[...], state)
    inv = lax.rsqrt(jnp.mean(att * att, axis=-1, keepdims=True) + 1e-05)
    normed = att * inv
    g = g_ref[...].astype(F32)
    low = (inv * (g - normed * jnp.mean(g * normed, axis=-1, keepdims=True))).astype(BF16)
    low_ref[...] = low
    local_ref[...] = dot(q_ref[...], low, TN).astype(BF16)


def norm_step(q, g, a, near, far):
    tok, cols = q.shape
    return pl.pallas_call(
        norm_kernel,
        out_shape=(sds((tok, cols), BF16), sds((cols, HDIM), BF16), sds((cols, HDIM), BF16)),
        grid=(cols // HDIM,),
        in_specs=[head_spec(tok)] * 3 + [state_spec()] * 2,
        out_specs=(head_spec(tok), state_spec(), state_spec()),
        compiler_params=params(),
        cost_estimate=cost(4 * tok * cols * HDIM, 10 * tok * cols),
        name="norm_grad",
    )(q, g, a, near, far)


def cross_kernel(q_ref, k_ref, v_ref, low_ref, state_ref, qg_ref, kp_ref, vp_ref):
    low = low_ref[...]
    c = tril(dot(low, v_ref[...], NT))
    qg_ref[...] = (dot(c, k_ref[...]) + dot(low, state_ref[...], NT)).astype(BF16)
    kp_ref[...] = dot(c, q_ref[...], TN)
    m = tril(dot(q_ref[...], k_ref[...], NT))
    vp_ref[...] = dot(m, low, TN)


def cross_step(q, k, v, low, state):
    tok, cols = q.shape
    return pl.pallas_call(
        cross_kernel,
        out_shape=(sds((tok, cols), BF16), sds((tok, cols), F32), sds((tok, cols), F32)),
        grid=(cols // HDIM,),
        in_specs=[head_spec(tok)] * 4 + [state_spec()],
        out_specs=(head_spec(tok),) * 3,
        compiler_params=params(),
        cost_estimate=cost(10 * tok * tok * cols, 18 * tok * cols),
        name="cross",
    )(q, k, v, low, state)


def fold_x_kernel(keep, mine_ref, a_ref, b_ref, c_ref, _, before_ref, *msgs):
    before = a_ref[...].astype(F32) + b_ref[...].astype(F32) + c_ref[...].astype(F32)
    before_ref[...] = before
    both = (before + mine_ref[...].astype(F32)).astype(BF16)
    alone = before.astype(BF16)
    for i, ref in enumerate(msgs):
        ref[...] = jnp.where(keep[i] > 0, both, alone)


def fold_y_kernel(ahead, mine_ref, before_ref, a_ref, b_ref, c_ref, near_ref, far_ref):
    near = before_ref[...] + (
        a_ref[...].astype(F32) + b_ref[...].astype(F32) + c_ref[...].astype(F32)
    )
    near_ref[...] = near
    more = near + mine_ref[...].astype(F32)
    far_ref[...] = jnp.where(ahead[0] > 0, more, near).astype(BF16)


def whole(shape):
    return pl.BlockSpec(shape, lambda s, *_: (0,) * len(shape))


def single(body, scalars, ins, specs, outs, flops=0, scratch=(), name=None, grid=1, out_specs=None):
    nbytes = sum(math.prod(o.shape) * o.dtype.itemsize for o in outs) * 2
    return pl.pallas_call(
        body,
        out_shape=tuple(outs),
        grid_spec=pltpu.PrefetchScalarGridSpec(
            num_scalar_prefetch=1,
            grid=(grid,),
            in_specs=specs,
            out_specs=out_specs or tuple(whole(o.shape) for o in outs),
            scratch_shapes=list(scratch),
        ),
        compiler_params=params(),
        cost_estimate=cost(flops, nbytes),
        name=name,
    )(scalars, *ins)


SIDE = 4


def along_x(a, k):
    return lax.ppermute(
        a, "ctx", [(i, i + SIDE * k) for i in range(16) if 0 <= i + SIDE * k < 16]
    )


def along_x_ring(a, k):
    return lax.ppermute(a, "ctx", [(i, (i + SIDE * k) % 16) for i in range(16)])


def along_y_ring(a, k):
    return lax.ppermute(
        a, "ctx", [(i, i // SIDE * SIDE + (i + k) % SIDE) for i in range(16)]
    )


def along_z(a, k):
    return lax.ppermute(a, "head", [(i, (i + k) % 8) for i in range(8)])


def swap(a):
    return lax.ppermute(a, "fsdp", [(0, 1), (1, 0)])


def exclusive(mine, keep, ahead, sign, work):
    shape = mine.shape
    got = [along_x(mine, sign * k) for k in (1, 2, 3)]
    done = work()
    before, *msgs = single(
        fold_x_kernel,
        keep,
        [mine, *got, jax.tree.leaves(done)[0]],
        [whole(shape)] * 4 + [ANY],
        [sds(shape, F32)] + [sds(shape, BF16)] * 3,
        name="fold_x",
    )
    got = [along_y_ring(m, sign * k) for m, k in zip(msgs, (1, 2, 3))]
    near, far = single(
        fold_y_kernel,
        ahead,
        [mine, before, *got],
        [whole(shape)] * 5,
        [sds(shape, F32), sds(shape, BF16)],
        name="fold_y",
    )
    return near, swap(far), done


def chunk_product(dests, vg, own_ref, other_ref, step, rows, use):
    core = dests[8]
    mine = dests[step] // 4 == core

    @pl.when(mine)
    def _():
        use(dot(vg, own_ref[...], NT).astype(BF16))

    @pl.when(jnp.logical_not(mine))
    def _():
        use(dot(vg, other_ref[...], NT).astype(BF16))


def first_kernel(dests, k_ref, vp_ref, near_ref, far_ref, own_ref, other_ref, vg_ref, state_ref, right_ref, left_ref):
    for h in range(k_ref.shape[1] // HDIM):
        cols = slice(h * HDIM, (h + 1) * HDIM)
        state = (near_ref[cols, :] + far_ref[cols, :].astype(F32)).astype(BF16)
        state_ref[cols, :] = state
        vg_ref[:, cols] = (vp_ref[:, cols] + dot(k_ref[:, cols], state)).astype(BF16)
    half = right_ref.shape[0]

    def use(p):
        right_ref[...] = p[:half]
        left_ref[...] = p[half:]

    chunk_product(dests, vg_ref[...], own_ref, other_ref, 0, 512, use)


def second_kernel(dests, vg_ref, own_ref, other_ref, rb_ref, la_ref, pa_ref, pb_ref):
    half = rb_ref.shape[0]
    step = pl.program_id(0)

    def use(p):
        @pl.when(step == 0)
        def _():
            pa_ref[...] = p[:half]
            rb_ref[...] = p[half:]

        @pl.when(step == 1)
        def _():
            la_ref[...] = p[:half]
            pb_ref[...] = p[half:]

    chunk_product(dests, vg_ref[...], own_ref, other_ref, 1 + step, 512, use)


def rest_kernel(dests, vg_ref, own_ref, other_ref, _, p_ref):
    def use(p):
        p_ref[0] = p

    chunk_product(dests, vg_ref[...], own_ref, other_ref, 3 + pl.program_id(0), 512, use)


def weight_chunk(first):
    return pl.BlockSpec((512, 512), lambda s, dests: (lax.rem(dests[first + s], 4), 0))


def turn_kernel(r_ref, l_ref, pr_ref, pl_ref, _, ro_ref, lo_ref):
    ro_ref[...] = (r_ref[...].astype(F32) + pr_ref[...].reshape(r_ref.shape).astype(F32)).astype(BF16)
    lo_ref[...] = (l_ref[...].astype(F32) + pl_ref[...].reshape(l_ref.shape).astype(F32)).astype(BF16)


def turn(r, l, pr, pr_at, pl_, pl_at, after):
    def part(at):
        if at is None:
            return pl.BlockSpec(r.shape, lambda s: (0, 0))
        return pl.BlockSpec((1,) + r.shape, lambda s: at + (0,))

    msg = pl.BlockSpec(r.shape, lambda s: (0, 0))
    return pl.pallas_call(
        turn_kernel,
        out_shape=(sds(r.shape, BF16),) * 2,
        grid=(1,),
        in_specs=[msg, msg, part(pr_at), part(pl_at), ANY],
        out_specs=(msg, msg),
        compiler_params=params(),
        cost_estimate=cost(0, 12 * r.size),
        name="turn",
    )(r, l, pr, pl_, after)


def last_kernel(p_ref, ra_ref, la_ref, rb_ref, lb_ref, _, o_ref):
    half = ra_ref.shape[0]
    p = p_ref[0].astype(F32)
    o_ref[:half] = (p[:half] + ra_ref[...].astype(F32) + la_ref[...].astype(F32)).astype(BF16)
    o_ref[half:] = (p[half:] + rb_ref[...].astype(F32) + lb_ref[...].astype(F32)).astype(BF16)


def last_turn(p, ra, la, rb, lb, after):
    _, tok, cols = p.shape
    msg = pl.BlockSpec(ra.shape, lambda s: (0, 0))
    return pl.pallas_call(
        last_kernel,
        out_shape=sds((tok, cols), BF16),
        grid=(1,),
        in_specs=[pl.BlockSpec((1, tok, cols), lambda s: (4, 0, 0)), msg, msg, msg, msg, ANY],
        out_specs=pl.BlockSpec((tok, cols), lambda s: (0, 0)),
        compiler_params=params(),
        cost_estimate=cost(0, 8 * tok * cols),
        name="last_turn",
    )(p, ra, la, rb, lb, after)


def key_grad_kernel(v_ref, kp_ref, state_ref, _, kg_ref):
    kg_ref[...] = (kp_ref[...] + dot(v_ref[...], state_ref[...], NT)).astype(BF16)


def key_grad_step(v, kp, state, after):
    tok, cols = v.shape
    return pl.pallas_call(
        key_grad_kernel,
        out_shape=sds((tok, cols), BF16),
        grid=(cols // HDIM,),
        in_specs=[head_spec(tok), head_spec(tok), state_spec(), ANY],
        out_specs=head_spec(tok),
        compiler_params=params(),
        cost_estimate=cost(2 * tok * cols * HDIM, 8 * tok * cols),
        name="key_grad",
    )(v, kp, state, after)


def weight_grad_kernel(scale, side, core, vg_ref, x_ref, _, o_ref, turned):
    @pl.when(pl.program_id(0) == 0)
    def _():
        turned[...] = vg_ref[...].T

    first = (core[0] == 0) if side == 0 else (core[0] == 1)
    x = x_ref[...]
    both = []
    for p in range(x.shape[1] // 256):
        a = x[:, p * 256 : p * 256 + 128]
        b = x[:, p * 256 + 128 : p * 256 + 256]
        both.append(jnp.where(first, a, b))
    res = dot(turned[...], jnp.concatenate(both, axis=1)) * scale
    for p in range(len(both)):
        o_ref[p] = res[:, p * 128 : p * 128 + 128].astype(BF16)


def weight_grad_step(core, vg, x, scale, side, after):
    tok, cols = vg.shape
    width = x.shape[1]
    pieces = width // 256

    def body(*refs):
        weight_grad_kernel(scale, side, *refs)

    return single(
        body,
        core,
        [vg, x, after],
        [whole((tok, cols)), pl.BlockSpec((tok, 1024), lambda s, core: (0, s)), ANY],
        [sds((pieces, cols, 128), BF16)],
        flops=tok * width * cols,
        scratch=[pltpu.VMEM((cols, tok), BF16)],
        name="weight_grad",
        grid=width // 1024,
        out_specs=(pl.BlockSpec((4, cols, 128), lambda s, core: (s, 0, 0)),),
    )[0]


def chip_kernel(where, a_ref, b_ref, _, ru2, lv2, rv1, lu1, cu1, cv1, own):
    s = (a_ref[0].astype(F32) + b_ref[0].astype(F32)).astype(BF16)
    half = s.shape[1] // 2
    step = pl.program_id(0)

    @pl.when(step == 0)
    def _():
        ru2[...] = s[:, :half]
        lv2[...] = s[:, half:]

    @pl.when(step == 1)
    def _():
        cu1[...] = s[:, :half]
        rv1[...] = s[:, half:]

    @pl.when(step == 2)
    def _():
        lu1[...] = s[:, :half]
        cv1[...] = s[:, half:]

    @pl.when(step == 3)
    def _():
        own[...] = s


def chip_step(where, mine, other, after):
    _, _, cols, width = mine.shape
    block = pl.BlockSpec((1, SIDE, cols, width), lambda s, where: (where[s], 0, 0, 0))
    piece = sds((SIDE, cols // 2, width), BF16)
    return single(
        chip_kernel,
        where,
        [mine, other, after],
        [block, block, ANY],
        [piece] * 6 + [sds((SIDE, cols, width), BF16)],
        name="chip",
        grid=4,
    )


def pair_kernel(_, a_ref, b_ref, c_ref, d_ref, _2, o_ref, p_ref):
    o_ref[...] = (a_ref[...].astype(F32) + b_ref[...].astype(F32)).astype(BF16)
    p_ref[...] = (c_ref[...].astype(F32) + d_ref[...].astype(F32)).astype(BF16)


def line_kernel(where, own_ref, ru_ref, lu_ref, rv_ref, lv_ref, _, m1, m2, m3, keep):
    own = own_ref[0].astype(F32)
    half = own.shape[0] // 2
    u = own[:half] + ru_ref[0].astype(F32) + lu_ref[0].astype(F32)
    v = own[half:] + rv_ref[0].astype(F32) + lv_ref[0].astype(F32)
    step = pl.program_id(0)
    for i, ref in enumerate((m1, m2, m3)):

        @pl.when(step == i)
        def _():
            ref[:half] = u.astype(BF16)
            ref[half:] = v.astype(BF16)

    @pl.when(step == 3)
    def _():
        keep[:half] = u
        keep[half:] = v


def line_step(where, own, ru, lu, rv, lv, after):
    _, cols, width = own.shape
    big = pl.BlockSpec((1, cols, width), lambda s, where: (where[4 + s], 0, 0))
    small = pl.BlockSpec((1, cols // 2, width), lambda s, where: (where[4 + s], 0, 0))
    return single(
        line_kernel,
        where,
        [own, ru, lu, rv, lv, after],
        [big] + [small] * 4 + [ANY],
        [sds((cols, width), BF16)] * 3 + [sds((cols, width), F32)],
        name="line",
        grid=4,
    )


def owner_kernel(_, keep_ref, a_ref, b_ref, c_ref, o_ref):
    t = keep_ref[...] + a_ref[...].astype(F32) + b_ref[...].astype(F32) + c_ref[...].astype(F32)
    o_ref[...] = t.T


def local(layer_input, query_act, key_act, out_grad, value_weight):
    tok, width = layer_input.shape
    cols = query_act.shape[1]
    core = lax.axis_index("fsdp")
    place = lax.axis_index("ctx")
    group = lax.axis_index("head")
    x, y = place // SIDE, lax.rem(place, SIDE)
    core_arr = core.reshape(1).astype(jnp.int32)
    hops = jnp.arange(1, 4, dtype=jnp.int32)
    onward = (y + hops < SIDE).astype(jnp.int32)
    back = (y - hops >= 0).astype(jnp.int32)
    dests = jnp.concatenate(
        [lax.rem(group + jnp.array([4, 3, 5, 2, 6, 1, 7, 0], jnp.int32), 8), core_arr]
    )
    where = jnp.concatenate(
        [
            lax.rem(x + jnp.array([2, 1, 3, 0], jnp.int32), SIDE),
            lax.rem(y + jnp.array([1, 2, 3, 0], jnp.int32), SIDE),
        ]
    )

    weight_other = swap(value_weight)
    part = value_own(core_arr, layer_input, value_weight)
    value, pair = value_rest(core_arr, layer_input, weight_other, part, key_act)
    near, far, attended = exclusive(
        pair, onward, 1 - core_arr, 1, lambda: inside(query_act, key_act, value)
    )
    low, state, own_grad = norm_step(query_act, out_grad, attended, near, far)
    near, far, (query_grad, key_part, value_part) = exclusive(
        own_grad, back, core_arr, -1, lambda: cross_step(query_act, key_act, value, low, state)
    )

    both_w = [value_weight, weight_other]
    msg = sds((tok // 2, 512), BF16)
    value_grad, state_grad, ra4, lb4 = single(
        first_kernel,
        dests,
        [key_act, value_part, near, far, *both_w],
        [whole((tok, cols))] * 2 + [whole((cols, HDIM))] * 2 + [weight_chunk(0)] * 2,
        [sds((tok, cols), BF16), sds((cols, HDIM), BF16), msg, msg],
        flops=4 * tok * cols * 512,
        name="value_grad",
    )
    ra4, lb4 = along_z(ra4, 1), along_z(lb4, -1)
    rb3, la3, pa3, pb3 = single(
        second_kernel,
        dests,
        [value_grad, *both_w],
        [whole((tok, cols))] + [weight_chunk(1)] * 2,
        [msg] * 4,
        flops=4 * tok * cols * 512,
        name="second",
        grid=2,
    )
    rb3, la3 = along_z(rb3, 1), along_z(la3, -1)

    seq_devices = lax.axis_size(("ctx", "fsdp"))
    scale = 1.0 / math.sqrt(tok * seq_devices)
    other = weight_grad_step(core_arr, value_grad, layer_input, scale, 1, pa3)
    got = swap(other)

    r, l = turn(ra4, lb4, pa3, None, pb3, None, other)
    ra3, lb3 = along_z(r, 1), along_z(l, -1)
    (rest,) = single(
        rest_kernel,
        dests,
        [value_grad, *both_w, r],
        [whole((tok, cols))] + [weight_chunk(3)] * 2 + [ANY],
        [sds((5, tok, 512), BF16)],
        flops=10 * tok * cols * 512,
        name="rest",
        grid=5,
        out_specs=(pl.BlockSpec((1, tok, 512), lambda s, dests: (s, 0, 0)),),
    )
    r, l = turn(rb3, la3, rest, (0, 1), rest, (1, 0), rest)
    rb2, la2 = along_z(r, 1), along_z(l, -1)
    mine = weight_grad_step(core_arr, value_grad, layer_input, scale, 0, r)
    r, l = turn(ra3, lb3, rest, (0, 0), rest, (1, 1), mine)
    ra2, lb2 = along_z(r, 1), along_z(l, -1)

    grid4 = (SIDE, SIDE) + mine.shape[1:]
    ru2, lv2, rv1, lu1, cu1, cv1, own = chip_step(
        where, mine.reshape(grid4), got.reshape(grid4), r
    )
    ru2, lv2 = along_x_ring(ru2, 1), along_x_ring(lv2, -1)
    rv1, lu1 = along_x_ring(rv1, 1), along_x_ring(lu1, -1)
    r, l = turn(rb2, la2, rest, (2, 1), rest, (3, 0), own)
    rb1, la1 = along_z(r, 1), along_z(l, -1)
    key_grad = key_grad_step(value, key_part, state_grad, r)
    r, l = turn(ra2, lb2, rest, (2, 0), rest, (3, 1), key_grad)
    ra1, lb1 = along_z(r, 1), along_z(l, -1)

    ru1, lv1 = single(
        pair_kernel,
        core_arr,
        [cu1, ru2, cv1, lv2, r],
        [whole(cu1.shape)] * 4 + [ANY],
        [sds(cu1.shape, BF16)] * 2,
        name="pair",
    )
    ru1, lv1 = along_x_ring(ru1, 1), along_x_ring(lv1, -1)
    m1, m2, m3, keep = line_step(where, own, ru1, lu1, rv1, lv1, lv1)
    got = [along_y_ring(m, k) for m, k in zip((m1, m2, m3), (1, 2, 3))]
    input_grad = last_turn(rest, ra1, la1, rb1, lb1, keep)
    (weight_grad,) = single(
        owner_kernel,
        core_arr,
        [keep, *got],
        [whole((cols, 128))] * 4,
        [sds((128, cols), F32)],
        name="owner",
    )
    return (query_grad, key_grad, input_grad, weight_grad)


def solution(mesh):
    in_specs = (
        P(("ctx", "fsdp"), None),
        P(("ctx", "fsdp"), "head"),
        P(("ctx", "fsdp"), "head"),
        P(("ctx", "fsdp"), "head"),
        P("fsdp", "head"),
    )
    out_specs = (
        P(("ctx", "fsdp"), "head"),
        P(("ctx", "fsdp"), "head"),
        P(("ctx", "fsdp"), "head"),
        P(("ctx", "fsdp"), "head"),
    )
    return jax.shard_map(local, mesh=mesh, in_specs=in_specs, out_specs=out_specs, check_vma=False)
```

time: 154 us -> 196 us (1.27)
  Pallas kernels: 26.3 us -> 91.9 us
  waiting for transfers between devices: 56.5 us -> 27.8 us
  starting transfers between devices: 30.7 us -> 57.1 us
  between operations: 14.4 us -> 0.94 us
  local copies, waits for them, and re-layouts: 18.3 us -> 14.3 us
  other arithmetic: 4.91 us -> 2.36 us
    pallas_call x3 -> x20, Pallas kernels: 12.6 us -> 66.3 us  [the longest x13 49 us: single(): pl.pallas_call(body, out_shape=tuple(outs), grid_spec=pltpu.PrefetchScala...]
    ppermute x0 -> x14, starting transfers between devices: none -> 23.2 us  [along_z(): return lax.ppermute(a, 'head', [(i, (i + k) % 8) for i in range(8)])]
    ppermute x3 -> x6, waiting for transfers between devices: 22.4 us -> 1.16 us  [along_x_ring(): return lax.ppermute(a, 'ctx', [(i, (i + SIDE * k) % 16) for i in range(16)])]
    ppermute x6, waiting for transfers between devices: 11.3 us -> 2.39 us  [along_x(): lax.ppermute(a, 'ctx', [(i, i + SIDE * k) for i in range(16) if 0 <= i +...]
    ppermute x0 -> x14, waiting for transfers between devices: none -> 5.94 us  [along_z(): return lax.ppermute(a, 'head', [(i, (i + k) % 8) for i in range(8)])]
    ppermute x3 -> x6, starting transfers between devices: 6.13 us -> 9.64 us  [along_x_ring(): return lax.ppermute(a, 'ctx', [(i, (i + SIDE * k) % 16) for i in range(16)])]
    dynamic_slice x4 -> x0, local copies, waits for them, and re-layouts: 3.27 us -> none  [pick(): return lax.dynamic_index_in_dim(a, lax.rem(place, SIDE), 0, False)]
    pallas_call x1, Pallas kernels: 2.77 us -> 5.84 us  [value_rest(): pl.pallas_call(value_rest_kernel, out_shape=(sds((tok, cols), BF16), sds(...]
  transfers between devices with their start and end apart: 23 -> 39, of which waited for: 15 -> 14; matrix products, arithmetic and copies ran while one was open for 5% -> 1% of each run, Pallas kernels for 11% -> 29%
where the time goes in v2:
time: 196 us; the launch traced here: 194 us
  Pallas kernels  91.9 us (47%)
  starting transfers between devices  57.1 us (29%)
  waiting for transfers between devices  27.8 us (14%)
  local copies, waits for them, and re-layouts  14.3 us (7%)
  other arithmetic  2.36 us (1%)
    pallas_call x13, Pallas kernels, single(): pl.pallas_call(body, out_shape=tuple(outs), grid_spec=pltpu.PrefetchScala...  49 us
    ppermute x14, starting transfers between devices, along_z(): return lax.ppermute(a, 'head', [(i, (i + k) % 8) for i in range(8)])  23.2 us
    ppermute x9, waiting for transfers between devices, along_y_ring(): lax.ppermute(a, 'ctx', [(i, i // SIDE * SIDE + (i + k) % SIDE) for i in r...  15.8 us
    unnamed x94, local copies, waits for them, and re-layouts  14.3 us
    ppermute x6, starting transfers between devices, along_x(): lax.ppermute(a, 'ctx', [(i, i + SIDE * k) for i in range(16) if 0 <= i +...  13.2 us
    ppermute x9, starting transfers between devices, along_y_ring(): lax.ppermute(a, 'ctx', [(i, i // SIDE * SIDE + (i + k) % SIDE) for i in r...  10.8 us
    pallas_call x5, Pallas kernels, turn(): pl.pallas_call(turn_kernel, out_shape=(sds(r.shape, BF16),) * 2, grid=(1,...  10.2 us
    ppermute x6, starting transfers between devices, along_x_ring(): return lax.ppermute(a, 'ctx', [(i, (i + SIDE * k) % 16) for i in range(16)])  9.64 us
  transfers between devices with their start and end apart: 39, of which 14 were waited for; matrix products, arithmetic and copies ran while one was open for 1% of the time, Pallas kernels for 29%

profile of v2, /device:TPU:24, one launch (start us, length us, event | category | flops | bytes accessed | tf_op | source)
XLA Modules:
  0.0 194.3 jit_solution(718483916090859811)
XLA Ops:
  0.7 5.1 %value_own.1.part_ref = f32[512,512]{1,0:T(8,128)} custom-call(s32[1]{0:T(128)} %bitcast.core.ahead.refs_0_._, bf16[512,4096]{1,0:T(8,128)(2,1)} %refs_2_.3, bf16[2048,512]{1,0:T(8,128)(2,1)} %own_ref.5), custom_call_target="tpu_custom_call" | custom-call | flops 1073741824 | bytes 4194304 | tf_op jit(solution)/shard_map/value_own/pallas_call | solution.py:50
  7.1 5.8 %value_rest.1 = (bf16[512,512]{1,0:T(8,128)(2,1)}, bf16[512,128]{1,0:T(8,128)(2,1)}) custom-call(s32[1]{0:T(128)} %bitcast.core.ahead.refs_0_._, bf16[512,4096]{1,0:T(8,128)(2,1)} %refs_2_.3, bf16[2048,512]{1,0:T(8,128)(2,1)} %copy-done, f32[512,512]{1,0:T(8,128)} %value_own.1.part_ref, bf16[512,512]{1,0:T(8,128)(2,1)} %k_ref.7), custom_call_target="tpu_custom_call" | custom-call | flops 1073741824 | bytes 4194304 | tf_op jit(solution)/shard_map/value_rest/pallas_call | solution.py:93
  13.0 3.4 %collective-permute-start.1 = (bf16[512,128]{1,0:T(8,128)(2,1)}, bf16[512,128]{1,0:T(8,128)(2,1)S(1)}, u32[]{:S(2)}, u32[]{:S(2)}) collective-permute-start(bf16[512,128]{1,0:T(8,128)(2,1)} %get-tuple-element.56.mine_ref), channel_id=1, source_target_pairs={{0,64},{16,80},{32,96},{48,112},{64,128},{80,144},{96,160},{112,17... | collective-permute-start | bytes 393224 | tf_op jit(solution)/shard_map/ppermute | solution.py:245
  16.4 4.6 %collective-permute-start.2 = (bf16[512,128]{1,0:T(8,128)(2,1)}, bf16[512,128]{1,0:T(8,128)(2,1)S(1)}, u32[]{:S(2)}, u32[]{:S(2)}) collective-permute-start(bf16[512,128]{1,0:T(8,128)(2,1)} %get-tuple-element.56.mine_ref), channel_id=1, source_target_pairs={{0,128},{16,144},{32,160},{48,176},{64,192},{80,208},{96,224},{112... | collective-permute-start | bytes 393224 | tf_op jit(solution)/shard_map/ppermute | solution.py:245
  22.8 4.7 %inside.1._.a_ref = f32[512,512]{1,0:T(8,128)} custom-call(bf16[512,512]{1,0:T(8,128)(2,1)} %q_ref.5, bf16[512,512]{1,0:T(8,128)(2,1)} %k_ref.7, bf16[512,512]{1,0:T(8,128)(2,1)} %get-tuple-element.55.v_ref), custom_call_target="tpu_custom_call" | custom-call | flops 536870912 | bytes 2621440 | tf_op jit(solution)/shard_map/inside/pallas_call | solution.py:140
  34.3 3.8 %collective-permute-done.4.a_ref = bf16[512,128]{1,0:T(8,128)(2,1)S(1)} collective-permute-done((bf16[512,128]{1,0:T(8,128)(2,1)}, bf16[512,128]{1,0:T(8,128)(2,1)S(1)}, u32[]{:S(2)}, u32[]{:S(2)}) %collective-permute-start.4) | collective-permute-done | bytes 131104 | tf_op jit(solution)/shard_map/ppermute | solution.py:255
  46.2 4.5 %norm_grad.1 = (bf16[512,512]{1,0:T(8,128)(2,1)}, bf16[512,128]{1,0:T(8,128)(2,1)}, bf16[512,128]{1,0:T(8,128)(2,1)}) custom-call(bf16[512,512]{1,0:T(8,128)(2,1)} %q_ref.5, bf16[512,512]{1,0:T(8,128)(2,1)} %g_ref.1, f32[512,512]{1,0:T(8,128)} %inside.1._.a_ref, f32[512,128]{1,0:T(8,128)} %get-tuple-element.61.near_ref, bf16[512,128]{1,0:T(8,128)(2,1)} %copy-done.30), custom_call_target="tpu_custom_call" | custom-call | flops 134217728 | bytes 2621440 | tf_op jit(solution)/shard_map/norm_grad/pallas_call | solution.py:166
  55.1 6.5 %cross.1 = (bf16[512,512]{1,0:T(8,128)(2,1)}, f32[512,512]{1,0:T(8,128)}, f32[512,512]{1,0:T(8,128)}) custom-call(bf16[512,512]{1,0:T(8,128)(2,1)} %q_ref.5, bf16[512,512]{1,0:T(8,128)(2,1)} %k_ref.7, bf16[512,512]{1,0:T(8,128)(2,1)} %get-tuple-element.55.v_ref, bf16[512,512]{1,0:T(8,128)(2,1)} %get-tuple-element.63.low_ref, ...), custom_call_target="tpu_custom_call" | custom-call | flops 1342177280 | bytes 4718592 | tf_op jit(solution)/shard_map/cross/pallas_call | solution.py:189
  71.6 4.3 %collective-permute-done.11.a_ref = bf16[512,128]{1,0:T(8,128)(2,1)S(1)} collective-permute-done((bf16[512,128]{1,0:T(8,128)(2,1)}, bf16[512,128]{1,0:T(8,128)(2,1)S(1)}, u32[]{:S(2)}, u32[]{:S(2)}) %collective-permute-start.11) | collective-permute-done | bytes 131104 | tf_op jit(solution)/shard_map/ppermute | solution.py:255
  81.2 4.3 %value_grad.1 = (bf16[512,512]{1,0:T(8,128)(2,1)}, bf16[512,128]{1,0:T(8,128)(2,1)}, bf16[256,512]{1,0:T(8,128)(2,1)}, bf16[256,512]{1,0:T(8,128)(2,1)}) custom-call(s32[9]{0:T(128)} %pad_add_fusion.dests, bf16[512,512]{1,0:T(8,128)(2,1)} %k_ref.7, f32[512,512]{1,0:T(8,128)} %get-tuple-element.67.vp_ref, f32[512,128]{1,0:T(8,128)} %get-tuple-element.73.near_ref, ...), custom_call_target="tpu_custom_call" | custom-call | flops 536870912 | bytes 2359296 | tf_op jit(solution)/shard_map/value_grad/pallas_call | solution.py:225
  85.5 4.2 %second.1 = (bf16[256,512]{1,0:T(8,128)(2,1)}, bf16[256,512]{1,0:T(8,128)(2,1)}, bf16[256,512]{1,0:T(8,128)(2,1)}, bf16[256,512]{1,0:T(8,128)(2,1)}) custom-call(s32[9]{0:T(128)} %pad_add_fusion.dests, bf16[512,512]{1,0:T(8,128)(2,1)} %get-tuple-element.76.vg_ref.refs_1_, bf16[2048,512]{1,0:T(8,128)(2,1)} %own_ref.5, bf16[2048,512]{1,0:T(8,128)(2,1)} %copy-done), custom_call_target="tpu_custom_call" | custom-call | flops 536870912 | bytes 2097152 | tf_op jit(solution)/shard_map/second/pallas_call | solution.py:225
  89.7 5.5 %weight_grad.2._ = bf16[16,512,128]{2,1,0:T(8,128)(2,1)} custom-call(s32[1]{0:T(128)} %bitcast.core.ahead.refs_0_._, bf16[512,512]{1,0:T(8,128)(2,1)} %get-tuple-element.76.vg_ref.refs_1_, bf16[512,4096]{1,0:T(8,128)(2,1)} %refs_2_.3, bf16[256,512]{1,0:T(8,128)(2,1)} %get-tuple-element.81.refs_3_.pr_ref), custom_call_target="tpu_custom_call" | custom-call | flops 1073741824 | bytes 4194304 | tf_op jit(solution)/shard_map/weight_grad/pallas_call | solution.py:225
  97.2 3.9 %collective-permute-start.18 = (bf16[256,512]{1,0:T(8,128)(2,1)}, bf16[256,512]{1,0:T(8,128)(2,1)S(1)}, u32[]{:S(2)}, u32[]{:S(2)}) collective-permute-start(bf16[256,512]{1,0:T(8,128)(2,1)} %get-tuple-element.80), channel_id=1, source_target_pairs={{0,14},{2,0},{4,2},{6,4},{8,6},{10,8},{12,10},{14,12},{1,15},{3,1}... | collective-permute-start | bytes 786440 | tf_op jit(solution)/shard_map/ppermute | solution.py:261
  101.2 3.2 %collective-permute-start.16 = (bf16[256,512]{1,0:T(8,128)(2,1)S(1)}, bf16[256,512]{1,0:T(8,128)(2,1)S(1)}, u32[]{:S(2)}, u32[]{:S(2)}) collective-permute-start(bf16[256,512]{1,0:T(8,128)(2,1)S(1)} %copy-done.44), channel_id=1, source_target_pairs={{0,14},{2,0},{4,2},{6,4},{8,6},{10,8},{12,10},{14,12},{1,15},{3,1}... | collective-permute-start | bytes 786440 | tf_op jit(solution)/shard_map/ppermute | solution.py:261
  104.4 4.0 %collective-permute-done.17.r_ref = bf16[256,512]{1,0:T(8,128)(2,1)S(1)} collective-permute-done((bf16[256,512]{1,0:T(8,128)(2,1)}, bf16[256,512]{1,0:T(8,128)(2,1)S(1)}, u32[]{:S(2)}, u32[]{:S(2)}) %collective-permute-start.17) | collective-permute-done | bytes 262176 | tf_op jit(solution)/shard_map/ppermute | solution.py:261
  111.2 7.2 %rest.1.pr_ref.pl_ref._.p_ref = bf16[5,512,512]{2,1,0:T(8,128)(2,1)} custom-call(s32[9]{0:T(128)} %pad_add_fusion.dests, bf16[512,512]{1,0:T(8,128)(2,1)} %get-tuple-element.76.vg_ref.refs_1_, bf16[2048,512]{1,0:T(8,128)(2,1)} %own_ref.5, bf16[2048,512]{1,0:T(8,128)(2,1)} %copy-done, bf16[256,512]{1,0:T(8,128)(2,1)} %get-tuple-element.83._), custom_call_target="tpu_custom_call" | custom-call | flops 1342177280 | bytes 5242880 | tf_op jit(solution)/shard_map/rest/pallas_call | solution.py:225
  121.9 3.0 %collective-permute-start.19 = (bf16[256,512]{1,0:T(8,128)(2,1)}, bf16[256,512]{1,0:T(8,128)(2,1)S(1)}, u32[]{:S(2)}, u32[]{:S(2)}) collective-permute-start(bf16[256,512]{1,0:T(8,128)(2,1)} %get-tuple-element.84.refs_3_), channel_id=1, source_target_pairs={{0,2},{2,4},{4,6},{6,8},{8,10},{10,12},{12,14},{14,0},{1,3},{3,5},... | collective-permute-start | bytes 786440 | tf_op jit(solution)/shard_map/ppermute | solution.py:261
  128.0 5.4 %weight_grad.3._ = bf16[16,512,128]{2,1,0:T(8,128)(2,1)} custom-call(s32[1]{0:T(128)} %bitcast.core.ahead.refs_0_._, bf16[512,512]{1,0:T(8,128)(2,1)} %get-tuple-element.76.vg_ref.refs_1_, bf16[512,4096]{1,0:T(8,128)(2,1)} %refs_2_.3, bf16[256,512]{1,0:T(8,128)(2,1)} %get-tuple-element.84.refs_3_), custom_call_target="tpu_custom_call" | custom-call | flops 1073741824 | bytes 4194304 | tf_op jit(solution)/shard_map/weight_grad/pallas_call | solution.py:225
  142.5 5.4 %chip.1 = (bf16[4,256,128]{2,1,0:T(8,128)(2,1)}, bf16[4,256,128]{2,1,0:T(8,128)(2,1)}, bf16[4,256,128]{2,1,0:T(8,128)(2,1)}, bf16[4,256,128]{2,1,0:T(8,128)(2,1)...) custom-call(s32[8]{0:T(128)} %pad_add_fusion.1.where, ...), custom_call_target="tpu_custom_call" | custom-call | bytes 4194304 | tf_op jit(solution)/shard_map/chip/pallas_call | solution.py:225
  148.5 3.7 %collective-permute-start.31 = (bf16[4,256,128]{2,1,0:T(8,128)(2,1)}, bf16[4,256,128]{2,1,0:T(8,128)(2,1)S(1)}, u32[]{:S(2)}, u32[]{:S(2)}) collective-permute-start(bf16[4,256,128]{2,1,0:T(8,128)(2,1)} %get-tuple-element.97), channel_id=1, source_target_pairs={{0,192},{16,208},{32,224},{48,240},{64,0},{80,16},{96,32},{112,48}... | collective-permute-start | bytes 786440 | tf_op jit(solution)/shard_map/ppermute | solution.py:251
  156.2 3.8 %key_grad.1._ = bf16[512,512]{1,0:T(8,128)(2,1)} custom-call(bf16[512,512]{1,0:T(8,128)(2,1)} %get-tuple-element.55.v_ref, f32[512,512]{1,0:T(8,128)} %get-tuple-element.66.kp_ref, bf16[512,128]{1,0:T(8,128)(2,1)} %get-tuple-element.75.state_ref, bf16[256,512]{1,0:T(8,128)(2,1)} %get-tuple-element.89._), custom_call_target="tpu_custom_call" | custom-call | flops 67108864 | bytes 2097152 | tf_op jit(solution)/shard_map/key_grad/pallas_call | solution.py:401
  166.4 3.1 %collective-permute-start.35 = (bf16[4,256,128]{2,1,0:T(8,128)(2,1)}, bf16[4,256,128]{2,1,0:T(8,128)(2,1)S(1)}, u32[]{:S(2)}, u32[]{:S(2)}) collective-permute-start(bf16[4,256,128]{2,1,0:T(8,128)(2,1)} %get-tuple-element.101), channel_id=1, source_target_pairs={{0,192},{16,208},{32,224},{48,240},{64,0},{80,16},{96,32},{112,48}... | collective-permute-start | bytes 786440 | tf_op jit(solution)/shard_map/ppermute | solution.py:251
  170.1 2.8 %collective-permute-start.27 = (bf16[256,512]{1,0:T(8,128)(2,1)S(1)}, bf16[256,512]{1,0:T(8,128)(2,1)S(1)}, u32[]{:S(2)}, u32[]{:S(2)}) collective-permute-start(bf16[256,512]{1,0:T(8,128)(2,1)S(1)} %copy-done.42), channel_id=1, source_target_pairs={{0,14},{2,0},{4,2},{6,4},{8,6},{10,8},{12,10},{14,12},{1,15},{3,1}... | collective-permute-start | bytes 786440 | tf_op jit(solution)/shard_map/ppermute | solution.py:261
  176.9 4.0 %line.1 = (bf16[512,128]{1,0:T(8,128)(2,1)}, bf16[512,128]{1,0:T(8,128)(2,1)}, bf16[512,128]{1,0:T(8,128)(2,1)}, f32[512,128]{1,0:T(8,128)}) custom-call(s32[8]{0:T(128)} %pad_add_fusion.1.where, bf16[4,512,128]{2,1,0:T(8,128)(2,1)} %get-tuple-element.88._.own_ref, bf16[4,256,128]{2,1,0:T(8,128)(2,1)} %copy-done.22, bf16[4,256,128]{2,1,0:T(8,128)(2,1)} %copy-done.20, ...), custom_call_target="tpu_custom_call" | custom-call | bytes 1310720 | tf_op jit(solution)/shard_map/line/pallas_call | solution.py:225
  (179 shorter events, 87.3 us)
Async XLA Ops:
  13.0 14.6 %collective-permute-start.1 = (bf16[512,128]{1,0:T(8,128)(2,1)}, bf16[512,128]{1,0:T(8,128)(2,1)S(1)}, u32[]{:S(2)}, u32[]{:S(2)}) collective-permute-start(bf16[512,128]{1,0:T(8,128)(2,1)} %get-tuple-element.56.mine_ref), channel_id=1, source_target_pairs={{0,64},{16,80},{32,96},{48,112},{64,128},{80,144},{96,160},{112,17... | collective-permute-start | bytes 393224 | tf_op jit(solution)/shard_map/ppermute | solution.py:245
  16.4 11.2 %collective-permute-start.2 = (bf16[512,128]{1,0:T(8,128)(2,1)}, bf16[512,128]{1,0:T(8,128)(2,1)S(1)}, u32[]{:S(2)}, u32[]{:S(2)}) collective-permute-start(bf16[512,128]{1,0:T(8,128)(2,1)} %get-tuple-element.56.mine_ref), channel_id=1, source_target_pairs={{0,128},{16,144},{32,160},{48,176},{64,192},{80,208},{96,224},{112... | collective-permute-start | bytes 393224 | tf_op jit(solution)/shard_map/ppermute | solution.py:245
  50.7 10.9 %collective-permute-start.8 = (bf16[512,128]{1,0:T(8,128)(2,1)}, bf16[512,128]{1,0:T(8,128)(2,1)S(1)}, u32[]{:S(2)}, u32[]{:S(2)}) collective-permute-start(bf16[512,128]{1,0:T(8,128)(2,1)} %get-tuple-element.68.mine_ref), channel_id=1, source_target_pairs={{64,0},{80,16},{96,32},{112,48},{128,64},{144,80},{160,96},{176,11... | collective-permute-start | bytes 393224 | tf_op jit(solution)/shard_map/ppermute | solution.py:245
  53.3 10.7 %collective-permute-start.10 = (bf16[512,128]{1,0:T(8,128)(2,1)}, bf16[512,128]{1,0:T(8,128)(2,1)S(1)}, u32[]{:S(2)}, u32[]{:S(2)}) collective-permute-start(bf16[512,128]{1,0:T(8,128)(2,1)} %get-tuple-element.68.mine_ref), channel_id=1, source_target_pairs={{192,0},{208,16},{224,32},{240,48},{193,1},{209,17},{225,33},{241,... | collective-permute-start | bytes 393224 | tf_op jit(solution)/shard_map/ppermute | solution.py:245
  95.2 46.0 %collective-permute-start.21 = (bf16[16,512,128]{2,1,0:T(8,128)(2,1)}, bf16[16,512,128]{2,1,0:T(8,128)(2,1)S(1)}, u32[]{:S(2)}, u32[]{:S(2)}) collective-permute-start(bf16[16,512,128]{2,1,0:T(8,128)(2,1)} %weight_grad.2._), channel_id=1, source_target_pairs={{0,1},{1,0},{2,3},{3,2},{4,5},{5,4},{6,7},{7,6},{8,9},{9,8},{10,11... | collective-permute-start | bytes 6291464 | tf_op jit(solution)/shard_map/ppermute | solution.py:265
  95.3 13.2 %collective-permute-start.17 = (bf16[256,512]{1,0:T(8,128)(2,1)}, bf16[256,512]{1,0:T(8,128)(2,1)S(1)}, u32[]{:S(2)}, u32[]{:S(2)}) collective-permute-start(bf16[256,512]{1,0:T(8,128)(2,1)} %get-tuple-element.79), channel_id=1, source_target_pairs={{0,2},{2,4},{4,6},{6,8},{8,10},{10,12},{12,14},{14,0},{1,3},{3,5},... | collective-permute-start | bytes 786440 | tf_op jit(solution)/shard_map/ppermute | solution.py:261
  97.2 11.2 %collective-permute-start.18 = (bf16[256,512]{1,0:T(8,128)(2,1)}, bf16[256,512]{1,0:T(8,128)(2,1)S(1)}, u32[]{:S(2)}, u32[]{:S(2)}) collective-permute-start(bf16[256,512]{1,0:T(8,128)(2,1)} %get-tuple-element.80), channel_id=1, source_target_pairs={{0,14},{2,0},{4,2},{6,4},{8,6},{10,8},{12,10},{14,12},{1,15},{3,1}... | collective-permute-start | bytes 786440 | tf_op jit(solution)/shard_map/ppermute | solution.py:261
  101.2 17.3 %collective-permute-start.15 = (bf16[256,512]{1,0:T(8,128)(2,1)}, bf16[256,512]{1,0:T(8,128)(2,1)S(1)}, u32[]{:S(2)}, u32[]{:S(2)}) collective-permute-start(bf16[256,512]{1,0:T(8,128)(2,1)} %get-tuple-element.77), channel_id=1, source_target_pairs={{0,2},{2,4},{4,6},{6,8},{8,10},{10,12},{12,14},{14,0},{1,3},{3,5},... | collective-permute-start | bytes 786440 | tf_op jit(solution)/shard_map/ppermute | solution.py:261
  101.2 17.3 %collective-permute-start.16 = (bf16[256,512]{1,0:T(8,128)(2,1)S(1)}, bf16[256,512]{1,0:T(8,128)(2,1)S(1)}, u32[]{:S(2)}, u32[]{:S(2)}) collective-permute-start(bf16[256,512]{1,0:T(8,128)(2,1)S(1)} %copy-done.44), channel_id=1, source_target_pairs={{0,14},{2,0},{4,2},{6,4},{8,6},{10,8},{12,10},{14,12},{1,15},{3,1}... | collective-permute-start | bytes 786440 | tf_op jit(solution)/shard_map/ppermute | solution.py:261
  111.2 22.1 %collective-permute-start.22 = (bf16[256,512]{1,0:T(8,128)(2,1)}, bf16[256,512]{1,0:T(8,128)(2,1)S(1)}, u32[]{:S(2)}, u32[]{:S(2)}) collective-permute-start(bf16[256,512]{1,0:T(8,128)(2,1)} %get-tuple-element.83._), channel_id=1, source_target_pairs={{0,2},{2,4},{4,6},{6,8},{8,10},{10,12},{12,14},{14,0},{1,3},{3,5},... | collective-permute-start | bytes 786440 | tf_op jit(solution)/shard_map/ppermute | solution.py:261
  121.9 26.5 %collective-permute-start.19 = (bf16[256,512]{1,0:T(8,128)(2,1)}, bf16[256,512]{1,0:T(8,128)(2,1)S(1)}, u32[]{:S(2)}, u32[]{:S(2)}) collective-permute-start(bf16[256,512]{1,0:T(8,128)(2,1)} %get-tuple-element.84.refs_3_), channel_id=1, source_target_pairs={{0,2},{2,4},{4,6},{6,8},{8,10},{10,12},{12,14},{14,0},{1,3},{3,5},... | collective-permute-start | bytes 786440 | tf_op jit(solution)/shard_map/ppermute | solution.py:261
  124.9 10.3 %collective-permute-start.23 = (bf16[256,512]{1,0:T(8,128)(2,1)S(1)}, bf16[256,512]{1,0:T(8,128)(2,1)S(1)}, u32[]{:S(2)}, u32[]{:S(2)}) collective-permute-start(bf16[256,512]{1,0:T(8,128)(2,1)S(1)} %copy-done.45), channel_id=1, source_target_pairs={{0,14},{2,0},{4,2},{6,4},{8,6},{10,8},{12,10},{14,12},{1,15},{3,1}... | collective-permute-start | bytes 786440 | tf_op jit(solution)/shard_map/ppermute | solution.py:261
  125.2 27.0 %collective-permute-start.20 = (bf16[256,512]{1,0:T(8,128)(2,1)}, bf16[256,512]{1,0:T(8,128)(2,1)S(1)}, u32[]{:S(2)}, u32[]{:S(2)}) collective-permute-start(bf16[256,512]{1,0:T(8,128)(2,1)} %get-tuple-element.85), channel_id=1, source_target_pairs={{0,14},{2,0},{4,2},{6,4},{8,6},{10,8},{12,10},{14,12},{1,15},{3,1}... | collective-permute-start | bytes 786440 | tf_op jit(solution)/shard_map/ppermute | solution.py:261
  137.9 22.0 %collective-permute-start.24 = (bf16[256,512]{1,0:T(8,128)(2,1)}, bf16[256,512]{1,0:T(8,128)(2,1)S(1)}, u32[]{:S(2)}, u32[]{:S(2)}) collective-permute-start(bf16[256,512]{1,0:T(8,128)(2,1)} %get-tuple-element.87._), channel_id=1, source_target_pairs={{0,2},{2,4},{4,6},{6,8},{8,10},{10,12},{12,14},{14,0},{1,3},{3,5},... | collective-permute-start | bytes 786440 | tf_op jit(solution)/shard_map/ppermute | solution.py:261
  139.7 20.5 %collective-permute-start.25 = (bf16[256,512]{1,0:T(8,128)(2,1)}, bf16[256,512]{1,0:T(8,128)(2,1)S(1)}, u32[]{:S(2)}, u32[]{:S(2)}) collective-permute-start(bf16[256,512]{1,0:T(8,128)(2,1)} %get-tuple-element.90), channel_id=1, source_target_pairs={{0,14},{2,0},{4,2},{6,4},{8,6},{10,8},{12,10},{14,12},{1,15},{3,1}... | collective-permute-start | bytes 786440 | tf_op jit(solution)/shard_map/ppermute | solution.py:261
  147.9 15.5 %collective-permute-start.30 = (bf16[4,256,128]{2,1,0:T(8,128)(2,1)}, bf16[4,256,128]{2,1,0:T(8,128)(2,1)S(1)}, u32[]{:S(2)}, u32[]{:S(2)}) collective-permute-start(bf16[4,256,128]{2,1,0:T(8,128)(2,1)} %get-tuple-element.95), channel_id=1, source_target_pairs={{0,64},{16,80},{32,96},{48,112},{64,128},{80,144},{96,160},{112,17... | collective-permute-start | bytes 786440 | tf_op jit(solution)/shard_map/ppermute | solution.py:251
  148.5 15.0 %collective-permute-start.31 = (bf16[4,256,128]{2,1,0:T(8,128)(2,1)}, bf16[4,256,128]{2,1,0:T(8,128)(2,1)S(1)}, u32[]{:S(2)}, u32[]{:S(2)}) collective-permute-start(bf16[4,256,128]{2,1,0:T(8,128)(2,1)} %get-tuple-element.97), channel_id=1, source_target_pairs={{0,192},{16,208},{32,224},{48,240},{64,0},{80,16},{96,32},{112,48}... | collective-permute-start | bytes 786440 | tf_op jit(solution)/shard_map/ppermute | solution.py:251
  152.2 17.9 %collective-permute-start.33 = (bf16[4,256,128]{2,1,0:T(8,128)(2,1)}, bf16[4,256,128]{2,1,0:T(8,128)(2,1)S(1)}, u32[]{:S(2)}, u32[]{:S(2)}) collective-permute-start(bf16[4,256,128]{2,1,0:T(8,128)(2,1)} %get-tuple-element.99), channel_id=1, source_target_pairs={{0,192},{16,208},{32,224},{48,240},{64,0},{80,16},{96,32},{112,48}... | collective-permute-start | bytes 786440 | tf_op jit(solution)/shard_map/ppermute | solution.py:251
  160.0 12.9 %collective-permute-start.34 = (bf16[4,256,128]{2,1,0:T(8,128)(2,1)S(1)}, bf16[4,256,128]{2,1,0:T(8,128)(2,1)S(1)}, u32[]{:S(2)}, u32[]{:S(2)}) collective-permute-start(bf16[4,256,128]{2,1,0:T(8,128)(2,1)S(1)} %copy-done.43), channel_id=1, source_target_pairs={{0,64},{16,80},{32,96},{48,112},{64,128},{80,144},{96,160},{112,17... | collective-permute-start | bytes 786440 | tf_op jit(solution)/shard_map/ppermute | solution.py:251
  166.4 9.8 %collective-permute-start.35 = (bf16[4,256,128]{2,1,0:T(8,128)(2,1)}, bf16[4,256,128]{2,1,0:T(8,128)(2,1)S(1)}, u32[]{:S(2)}, u32[]{:S(2)}) collective-permute-start(bf16[4,256,128]{2,1,0:T(8,128)(2,1)} %get-tuple-element.101), channel_id=1, source_target_pairs={{0,192},{16,208},{32,224},{48,240},{64,0},{80,16},{96,32},{112,48}... | collective-permute-start | bytes 786440 | tf_op jit(solution)/shard_map/ppermute | solution.py:251
  169.5 14.0 %collective-permute-start.26 = (bf16[256,512]{1,0:T(8,128)(2,1)}, bf16[256,512]{1,0:T(8,128)(2,1)S(1)}, u32[]{:S(2)}, u32[]{:S(2)}) collective-permute-start(bf16[256,512]{1,0:T(8,128)(2,1)} %get-tuple-element.91._2), channel_id=1, source_target_pairs={{0,2},{2,4},{4,6},{6,8},{8,10},{10,12},{12,14},{14,0},{1,3},{3,5},... | collective-permute-start | bytes 786440 | tf_op jit(solution)/shard_map/ppermute | solution.py:261
  170.1 14.0 %collective-permute-start.27 = (bf16[256,512]{1,0:T(8,128)(2,1)S(1)}, bf16[256,512]{1,0:T(8,128)(2,1)S(1)}, u32[]{:S(2)}, u32[]{:S(2)}) collective-permute-start(bf16[256,512]{1,0:T(8,128)(2,1)S(1)} %copy-done.42), channel_id=1, source_target_pairs={{0,14},{2,0},{4,2},{6,4},{8,6},{10,8},{12,10},{14,12},{1,15},{3,1}... | collective-permute-start | bytes 786440 | tf_op jit(solution)/shard_map/ppermute | solution.py:261
  172.9 11.7 %collective-permute-start.28 = (bf16[256,512]{1,0:T(8,128)(2,1)S(1)}, bf16[256,512]{1,0:T(8,128)(2,1)S(1)}, u32[]{:S(2)}, u32[]{:S(2)}) collective-permute-start(bf16[256,512]{1,0:T(8,128)(2,1)S(1)} %copy-done.3), channel_id=1, source_target_pairs={{0,2},{2,4},{4,6},{6,8},{8,10},{10,12},{12,14},{14,0},{1,3},{3,5},... | collective-permute-start | bytes 786440 | tf_op jit(solution)/shard_map/ppermute | solution.py:261
  174.1 10.4 %collective-permute-start.29 = (bf16[256,512]{1,0:T(8,128)(2,1)}, bf16[256,512]{1,0:T(8,128)(2,1)S(1)}, u32[]{:S(2)}, u32[]{:S(2)}) collective-permute-start(bf16[256,512]{1,0:T(8,128)(2,1)} %get-tuple-element.93), channel_id=1, source_target_pairs={{0,14},{2,0},{4,2},{6,4},{8,6},{10,8},{12,10},{14,12},{1,15},{3,1}... | collective-permute-start | bytes 786440 | tf_op jit(solution)/shard_map/ppermute | solution.py:261
  (62 other events, 236.1 us)
